TPU v7x, 512 devices: a whole 4x8x8 slice. The times are simulated.
512 devices in a mesh: rows: 128 (over y, z, core), sub: 4 (over x).
Axes of the slice: x: 4, y: 8, z: 8, core: 2. Of those that a mesh axis runs over, the one named last changes fastest.
Arguments:
- slab: float32 [131072, 1024], P(('rows', 'sub')), may hold values from -150 to 150
- test_matrix: float32 [1024, 72], replicated, may hold values from -6 to 6
Outputs:
- row_factor: float32 [131072, 72], P(('rows', 'sub'))
- projected: float32 [72, 1024], replicated
All inputs are finite; a program needn't handle non-finite values.
Results may differ from a plain program's by a relative error of at most 0.0001.
Values sent between devices are 32-bit elements; how exact they have to be, the bound alone decides.
No kernel may reach another device: no remote copies, remote signals or barrier semaphores. Data moves between devices by JAX's collectives and lax.ppermute only.
A program may use at most 64 MiB of HBM per device.

v0:
```python
import math

import jax
import jax.numpy as jnp
from jax import lax
from jax.sharding import PartitionSpec as P

ITERS = 2


HI = lax.Precision.HIGHEST


def inverse_factor(gram):
    low = jnp.linalg.cholesky(gram)
    eye = jnp.eye(gram.shape[0], dtype=jnp.float32)
    return lax.linalg.triangular_solve(low, eye, left_side=True, lower=True)


def local_gram(block):
    return jnp.einsum("mk,ml->kl", block, block, precision=HI)


def orthonormal(block):
    return jnp.dot(block, inverse_factor(local_gram(block)).T, precision=HI)


def reduce_cross(terms):
    return lax.psum(terms, ("rows", "sub"))


def factor_and_cross(slab, sampled):
    gram_sum = lax.psum(local_gram(sampled), ("rows", "sub"))
    factor = jnp.dot(sampled, inverse_factor(gram_sum).T, precision=HI)
    cross = reduce_cross(jnp.einsum("md,mk->dk", slab, factor, precision=HI))
    return (factor, cross)


def local(slab, test_matrix):
    scale = math.sqrt(slab.shape[0] * lax.axis_size("rows") * lax.axis_size("sub"))
    current = test_matrix
    for step in range(ITERS + 1):
        sampled = jnp.dot(slab, current, precision=HI)
        factor, cross = factor_and_cross(slab, sampled)
        if step < ITERS:
            current = orthonormal(cross)
    return (factor * scale, cross.T / scale)


def solution(mesh):
    in_specs = (P(("rows", "sub"), None), P())
    out_specs = (P(("rows", "sub"), None), P())
    return jax.shard_map(local, mesh=mesh, in_specs=in_specs, out_specs=out_specs, check_vma=False)
```

profile of v0, /device:TPU:1, one launch (start us, length us, event | category | flops | bytes accessed | tf_op | source)
XLA Modules:
  0.0 1190.3 jit_solution(8192486615501342334)
XLA Ops:
  7.2 1.2 copy-done
  8.4 2.0 fusion.25
  10.4 0.2 fusion.26
  10.7 106.2 %psum.42 = f32[72,72]{0,1:T(8,128)S(1)} all-reduce(f32[72,72]{0,1:T(8,128)S(1)} %fusion.26), channel_id=1, replica_groups=mesh['rows'=128,'sub'=4] {'rows','sub'}, use_global_device_ids=true, to_apply=%region_0.0 | all-reduce | flops 5184 | bytes 41472 | tf_op jit(solution)/shard_map/psum | solution.py:33
  117.0 6.6 cholesky.89
  123.6 0.6 compare_reduce_fusion.4
  124.2 0.7 fusion.10
  124.9 5.5 custom-call.9
  130.4 0.3 fusion.8
  130.7 0.4 fusion.27
  131.1 1.5 convolution_bitcast_fusion.2
  132.7 261.9 %all-reduce.4.cloned.1.call-done = f32[1024,72]{0,1:T(8,128)} async-done(((f32[1024,72]{0,1:T(8,128)}), f32[1024,72]{0,1:T(8,128)}) %all-reduce.4.cloned.1.call-update) | async-done | bytes 294928 | tf_op jit(solution)/shard_map/psum | solution.py:29
  394.6 1.4 fusion.28
  396.1 6.6 cholesky.100
  402.7 0.6 compare_reduce_fusion.3
  403.4 0.7 fusion.11
  404.0 5.5 custom-call.10
  409.6 0.3 fusion.6
  409.8 1.0 fusion.29
  410.9 1.0 fusion.30
  411.9 0.2 fusion.31
  412.1 96.3 %psum.44 = f32[72,72]{0,1:T(8,128)S(1)} all-reduce(f32[72,72]{0,1:T(8,128)S(1)} %fusion.31), channel_id=1, replica_groups=mesh['rows'=128,'sub'=4] {'rows','sub'}, use_global_device_ids=true, to_apply=%region_4.7 | all-reduce | flops 5184 | bytes 41472 | tf_op jit(solution)/shard_map/psum | solution.py:33
  508.5 6.6 cholesky.111
  515.1 0.6 compare_reduce_fusion.2
  515.7 0.7 fusion.12
  516.4 5.5 custom-call.11
  521.9 0.3 fusion.4
  522.2 0.4 fusion.32
  522.6 1.5 convolution_bitcast_fusion.1
  524.1 263.9 %all-reduce.6.cloned.1.call-done = f32[1024,72]{0,1:T(8,128)} async-done(((f32[1024,72]{0,1:T(8,128)}), f32[1024,72]{0,1:T(8,128)}) %all-reduce.6.cloned.1.call-update) | async-done | bytes 294928 | tf_op jit(solution)/shard_map/psum | solution.py:29
  788.1 1.4 fusion.33
  789.6 6.6 cholesky.122
  796.3 0.6 compare_reduce_fusion.1
  796.9 0.7 fusion.13
  797.6 5.5 custom-call.12
  803.1 0.3 fusion.2
  803.4 1.0 fusion.34
  804.4 1.0 fusion.35
  805.6 96.3 %psum.46 = f32[72,72]{0,1:T(8,128)S(1)} all-reduce(f32[72,72]{0,1:T(8,128)S(1)} %fusion.36), channel_id=1, replica_groups=mesh['rows'=128,'sub'=4] {'rows','sub'}, use_global_device_ids=true, to_apply=%region_6.9 | all-reduce | flops 5184 | bytes 41472 | tf_op jit(solution)/shard_map/psum | solution.py:33
  902.0 6.6 cholesky.133
  908.6 0.6 compare_reduce_fusion
  909.3 0.7 fusion.14
  909.9 5.5 custom-call.13
  915.5 0.3 fusion
  915.7 0.8 broadcast_multiply_fusion
  916.6 1.5 convolution_bitcast_fusion
  918.1 264.0 %all-reduce.8.cloned.1.call-done = f32[1024,72]{0,1:T(8,128)} async-done(((f32[1024,72]{0,1:T(8,128)}), f32[1024,72]{0,1:T(8,128)}) %all-reduce.8.cloned.1.call-update) | async-done | bytes 294928 | tf_op jit(solution)/shard_map/psum | solution.py:29
  1182.1 1.7 multiply_bitcast_fusion
  (27 shorter events, 1.0 us)
Async XLA Ops:
  7.2 1.2 copy-start
  7.2 387.4 %all-reduce.4.cloned.1.call-start = ((), (), s32[]{:S(2)}) async-start(), calls=%async_computation | async-start | bytes 589824 | tf_op jit(solution)/shard_map/psum | solution.py:29
  132.6 655.5 %all-reduce.6.cloned.1.call-start = ((), (), s32[]{:S(2)}) async-start(), calls=%async_computation.1 | async-start | bytes 589824 | tf_op jit(solution)/shard_map/psum | solution.py:29
  396.0 13.8 %copy-start.1 = (f32[1024,72]{0,1:T(8,128)S(1)}, f32[1024,72]{0,1:T(8,128)}, u32[]{:S(2)}) copy-start(f32[1024,72]{0,1:T(8,128)} %all-reduce.4.cloned.1.call-done) | copy-start | bytes 884740
  524.1 658.0 %all-reduce.8.cloned.1.call-start = ((), (), s32[]{:S(2)}) async-start(), calls=%async_computation.2 | async-start | bytes 589824 | tf_op jit(solution)/shard_map/psum | solution.py:29
  789.5 13.8 %copy-start.2 = (f32[1024,72]{0,1:T(8,128)S(1)}, f32[1024,72]{0,1:T(8,128)}, u32[]{:S(2)}) copy-start(f32[1024,72]{0,1:T(8,128)} %all-reduce.6.cloned.1.call-done) | copy-start | bytes 884740
Sparse Core Ops, SparseCore 0:
  132.7 261.8 all-reduce.3
  524.2 263.8 all-reduce.5
  918.2 263.8 all-reduce.7
where the time goes:
time: 1190 us
  waiting for transfers between devices  790 us (66%)
  blocking collectives  299 us (25%)
  other arithmetic  68.9 us (6%)
  matrix products  16.9 us (1%)
  between operations  14.1 us (1%)
    psum x3, waiting for transfers between devices, reduce_cross(): return lax.psum(terms, ('rows', 'sub'))  790 us
    psum x3, blocking collectives, factor_and_cross(): gram_sum = lax.psum(local_gram(sampled), ('rows', 'sub'))  299 us
    another operation x15, other arithmetic, inverse_factor(): low = jnp.linalg.cholesky(gram)  36.3 us
    another operation x10, other arithmetic, inverse_factor(): return lax.linalg.triangular_solve(low, eye, left_side=True, lower=True)  30.9 us
  transfers between devices with their start and end apart: 3, of which 3 were waited for; matrix products, arithmetic and copies ran while one was open for 0% of the time, Pallas kernels for 0%

commit v1 on v0

v1 whole, which is shorter than its diff:
```python
import functools
import math

import jax
import jax.numpy as jnp
from jax import lax
from jax.experimental import pallas as pl
from jax.experimental.pallas import tpu as pltpu
from jax.sharding import Mesh, PartitionSpec as P

ITERS = 2
HI = lax.Precision.HIGHEST
B = 128
VMEM_LIMIT = 56 * 1024 * 1024

NT = (((1,), (1,)), ((), ()))
NN = (((1,), (0,)), ((), ()))


def dot(a, b, dims=NN):
    return lax.dot_general(a, b, dims, precision=HI, preferred_element_type=jnp.float32)


def block_pairs(n):
    return [(i, j) for i in range(n) for j in range(i, n)]


def gram_kernel(core_ref, a_ref, out_ref, at_ref):
    n = a_ref.shape[1] // B
    core = core_ref[0]
    at_ref[...] = a_ref[...].T
    pairs = block_pairs(n)
    half = len(pairs) // 2
    place = {pair: index for index, pair in enumerate(pairs)}
    for i in range(n):
        row = dot(at_ref[i * B:(i + 1) * B, :], a_ref[:, i * B:])
        for j in range(i, n):
            index = place[(i, j)]
            slot = core if index < half else 1 - core
            start = (index % half) * B
            out_ref[slot, start:start + B, :] = row[:, (j - i) * B:(j - i + 1) * B]


def local_gram(core, a):
    n = a.shape[1] // B
    half = n * (n + 1) // 4
    return pl.pallas_call(
        gram_kernel,
        out_shape=jax.ShapeDtypeStruct((2, half * B, B), jnp.float32),
        in_specs=[
            pl.BlockSpec(memory_space=pltpu.SMEM),
            pl.BlockSpec(memory_space=pltpu.VMEM),
        ],
        out_specs=pl.BlockSpec(memory_space=pltpu.VMEM),
        scratch_shapes=[pltpu.VMEM((a.shape[1], a.shape[0]), jnp.float32)],
        compiler_params=pltpu.CompilerParams(vmem_limit_bytes=VMEM_LIMIT),
        name="local_gram",
    )(core, a)


def inverse_factor(gram):
    k = gram.shape[0]
    rows = k // 8
    wide = jnp.concatenate([gram, jnp.zeros((k, B - k), jnp.float32)], axis=1)
    tiles = [wide[8 * t:8 * t + 8, :] for t in range(rows)]
    lane = lax.broadcasted_iota(jnp.int32, (8, B), 1)
    sub = lax.broadcasted_iota(jnp.int32, (8, B), 0)
    scale = []
    for j in range(k):
        t, s = divmod(j, 8)
        row = tiles[t][s:s + 1, :]
        pivot = row[:, j:j + 1]
        row = jnp.where(lane[0:1, :] == j, 1.0, row) * (1.0 / pivot)
        scale.append(lax.rsqrt(pivot))
        for u in range(t, rows):
            column = jnp.broadcast_to(tiles[u][:, j:j + 1], (8, B))
            rest = jnp.where(lane == j, 0.0, tiles[u])
            new = rest - column * row
            tiles[u] = jnp.where(sub > s, new, tiles[u]) if u == t else new
    out = []
    for t in range(rows):
        below = jnp.where(lane < sub + 8 * t, tiles[t], 0.0)
        below = jnp.where(lane == sub + 8 * t, 1.0, below)
        out.append(below * jnp.concatenate(scale[8 * t:8 * t + 8], axis=0))
    return jnp.concatenate(out, axis=0)[:, :k]


def iterate_kernel(total, core_ref, own_ref, other_ref, xt_ref, a_ref, row_ref, proj_ref, c_ref):
    n = c_ref.shape[0] // B
    core = core_ref[0]
    pairs = block_pairs(n)
    half = len(pairs) // 2
    for index, (i, j) in enumerate(pairs):
        start = (index % half) * B
        own, other = own_ref[start:start + B, :], other_ref[start:start + B, :]
        mine = (core == 0) if index < half else (core == 1)
        block = jnp.where(mine, own, other)
        c_ref[i * B:(i + 1) * B, j * B:(j + 1) * B] = block
        if i < j:
            c_ref[j * B:(j + 1) * B, i * B:(i + 1) * B] = block.T
    root = math.sqrt(total)
    xt = xt_ref[...]
    for step in range(ITERS + 1):
        zt = dot(xt, c_ref[...])
        inv = inverse_factor(dot(xt, zt, NT))
        crosst = dot(inv, zt)
        if step < ITERS:
            xt = dot(inverse_factor(dot(crosst, crosst, NT)), crosst)
    proj_ref[...] = crosst / root
    y = dot(a_ref[...], xt, NT)
    row_ref[...] = dot(y, inv, NT) * root


def iterate(total, core, own, other, xt, a):
    k, d = xt.shape
    vmem = pl.BlockSpec(memory_space=pltpu.VMEM)
    return pl.pallas_call(
        functools.partial(iterate_kernel, total),
        out_shape=(
            jax.ShapeDtypeStruct((a.shape[0], k), jnp.float32),
            jax.ShapeDtypeStruct((k, d), jnp.float32),
        ),
        in_specs=[pl.BlockSpec(memory_space=pltpu.SMEM)] + [vmem] * 4,
        out_specs=(vmem, vmem),
        scratch_shapes=[pltpu.VMEM((d, d), jnp.float32)],
        compiler_params=pltpu.CompilerParams(vmem_limit_bytes=VMEM_LIMIT),
        name="iterate",
    )(core, own, other, xt, a)


def scatter_sum(v, axes):
    return jnp.sum(lax.all_to_all(v, axes, 0, 0, tiled=True), axis=0)


def collect(v, axes):
    copies = jnp.broadcast_to(v[None], (lax.axis_size(axes),) + v.shape)
    return lax.all_to_all(copies, axes, 0, 0, tiled=True)


def all_sum(v):
    cut = 40 * 32
    first = scatter_sum(v[:cut].reshape(32, -1, B), ("z", "x"))
    second = scatter_sum(v[cut:].reshape(32, -1, B), ("y", "x"))
    first = jnp.sum(collect(first, "y"), axis=0)
    second = jnp.sum(collect(second, "z"), axis=0)
    first = collect(first, ("z", "x"))
    second = collect(second, ("y", "x"))
    return jnp.concatenate([first.reshape(-1, B), second.reshape(-1, B)], axis=0)


def swap(v):
    return lax.ppermute(v, "core", [(0, 1), (1, 0)])


def local(total, slab, test_matrix):
    core = lax.axis_index("core").astype(jnp.int32)[None]
    parts = local_gram(core, slab)
    own = all_sum(parts[0] + swap(parts[1]))
    other = swap(own)
    return iterate(total, core, own, other, test_matrix.T, slab)


def solution(mesh):
    fine = Mesh(mesh.devices.reshape(8, 8, 2, 4), ("y", "z", "core", "x"))
    split = P(("y", "z", "core", "x"), None)

    def run(slab, test_matrix):
        return jax.shard_map(
            functools.partial(local, slab.shape[0]),
            mesh=fine,
            in_specs=(split, P()),
            out_specs=(split, P()),
            check_vma=False,
        )(slab, test_matrix)

    return run
```

time: 1190 us -> 190 us (0.16)
  waiting for transfers between devices: 790 us -> 66.9 us
  blocking collectives: 299 us -> 17.4 us
  other arithmetic: 68.9 us -> 0.33 us
  Pallas kernels: 0 us -> 49.1 us
  starting transfers between devices: 0.12 us -> 46.7 us
  matrix products: 16.9 us -> 0 us
  between operations: 14.1 us -> 0.72 us
    psum x3 -> x0, waiting for transfers between devices: 790 us -> none  [reduce_cross(): return lax.psum(terms, ('rows', 'sub'))]
    psum x3 -> x0, blocking collectives: 299 us -> none  [factor_and_cross(): gram_sum = lax.psum(local_gram(sampled), ('rows', 'sub'))]
    another operation x25 -> x0, other arithmetic: 67.1 us -> none  [the longest x15 36.3 us: inverse_factor(): low = jnp.linalg.cholesky(gram)]
    all_to_all x0 -> x5, waiting for transfers between devices: none -> 62.2 us  [the longest x2 33.2 us: scatter_sum(): return jnp.sum(lax.all_to_all(v, axes, 0, 0, tiled=True), axis=0)]
    pallas_call x0 -> x2, Pallas kernels: none -> 49.1 us  [the longest x1 44 us: iterate(): pl.pallas_call(functools.partial(iterate_kernel, total), out_shape=(jax.S...]
    all_to_all x0 -> x5, starting transfers between devices: none -> 28 us  [the longest x2 16.7 us: scatter_sum(): return jnp.sum(lax.all_to_all(v, axes, 0, 0, tiled=True), axis=0)]
    ppermute x0 -> x2, starting transfers between devices: none -> 18.7 us  [swap(): return lax.ppermute(v, 'core', [(0, 1), (1, 0)])]
    all_to_all x0 -> x1, blocking collectives: none -> 17.4 us  [collect(): return lax.all_to_all(copies, axes, 0, 0, tiled=True)]
  transfers between devices with their start and end apart: 3 -> 7, of which waited for: 3 -> 7; matrix products, arithmetic and copies ran while one was open for 0% -> 1% of each run, Pallas kernels for 0% -> 0%
where the time goes in v1:
time: 190 us; the launch traced here: 189 us
  waiting for transfers between devices  66.9 us (35%)
  Pallas kernels  49.1 us (26%)
  starting transfers between devices  46.7 us (25%)
  blocking collectives  17.4 us (9%)
  local copies, waits for them, and re-layouts  8.12 us (4%)
    pallas_call x1, Pallas kernels, iterate(): pl.pallas_call(functools.partial(iterate_kernel, total), out_shape=(jax.S...  44 us
    all_to_all x2, waiting for transfers between devices, scatter_sum(): return jnp.sum(lax.all_to_all(v, axes, 0, 0, tiled=True), axis=0)  33.2 us
    all_to_all x3, waiting for transfers between devices, collect(): return lax.all_to_all(copies, axes, 0, 0, tiled=True)  29 us
    ppermute x2, starting transfers between devices, swap(): return lax.ppermute(v, 'core', [(0, 1), (1, 0)])  18.7 us
    all_to_all x1, blocking collectives, collect(): return lax.all_to_all(copies, axes, 0, 0, tiled=True)  17.4 us
    all_to_all x2, starting transfers between devices, scatter_sum(): return jnp.sum(lax.all_to_all(v, axes, 0, 0, tiled=True), axis=0)  16.7 us
    all_to_all x3, starting transfers between devices, collect(): return lax.all_to_all(copies, axes, 0, 0, tiled=True)  11.3 us
    pallas_call x1, Pallas kernels, local_gram(): pl.pallas_call(gram_kernel, out_shape=jax.ShapeDtypeStruct((2, half * B,...  5.14 us
  transfers between devices with their start and end apart: 7, of which 7 were waited for; matrix products, arithmetic and copies ran while one was open for 1% of the time, Pallas kernels for 0%

profile of v1, /device:TPU:1, one launch (start us, length us, event | category | flops | bytes accessed | tf_op | source)
XLA Modules:
  0.0 189.3 jit_solution(9919615136214832497)
XLA Ops:
  0.6 5.1 %local_gram.1 = f32[2,2304,128]{2,1,0:T(8,128)} custom-call(s32[1]{0:T(128)} %bitcast.core_ref, f32[256,1024]{1,0:T(8,128)} %a_ref.3), custom_call_target="tpu_custom_call" | custom-call | tf_op jit(solution)/shard_map/local_gram/pallas_call | solution.py:47
  5.8 0.0 copy-start
  5.8 1.5 slice_bitcast_fusion
  7.3 8.8 %collective-permute-start = (f32[2304,128]{1,0:T(8,128)S(1)}, f32[2304,128]{1,0:T(8,128)S(1)}, u32[]{:S(2)}, u32[]{:S(2)}) collective-permute-start(f32[2304,128]{1,0:T(8,128)S(1)} %slice_bitcast_fusion), channel_id=1, source_target_pairs={{0,4},{4,0},{1,5},{5,1},{2,6},{6,2},{3,7},{7,3},{8,12},{12,8},{9,1... | collective-permute-start | bytes 3538952 | tf_op jit(solution)/shard_map/ppermute | solution.py:152
  16.1 2.5 %collective-permute-done = f32[2304,128]{1,0:T(8,128)S(1)} collective-permute-done((f32[2304,128]{1,0:T(8,128)S(1)}, f32[2304,128]{1,0:T(8,128)S(1)}, u32[]{:S(2)}, u32[]{:S(2)}) %collective-permute-start) | collective-permute-done | bytes 1179680 | tf_op jit(solution)/shard_map/ppermute | solution.py:152
  18.5 0.0 copy-done
  18.5 0.1 fusion
  18.7 0.8 slice.19
  19.5 4.3 %all-to-all-start.3 = ((f32[32,32,128]{2,1,0:T(8,128)}), f32[32,32,128]{2,1,0:T(8,128)S(1)}, u32[]{:S(2)}, u32[]{:S(2)}) async-start(f32[32,32,128]{2,1,0:T(8,128)} %bitcast.5), calls=%async_computation.3 | async-start | bytes 1048576 | tf_op jit(solution)/shard_map/all_to_all | solution.py:132
  23.8 0.9 slice.18
  24.7 15.7 %all-to-all-done.3 = f32[32,32,128]{2,1,0:T(8,128)S(1)} async-done(((f32[32,32,128]{2,1,0:T(8,128)}), f32[32,32,128]{2,1,0:T(8,128)S(1)}, u32[]{:S(2)}, u32[]{:S(2)}) %all-to-all-start.3) | async-done | bytes 524320 | tf_op jit(solution)/shard_map/all_to_all | solution.py:132
  40.4 12.4 %all-to-all-start = ((f32[32,40,128]{2,1,0:T(8,128)}), f32[32,40,128]{2,1,0:T(8,128)S(1)}, u32[]{:S(2)}, u32[]{:S(2)}) async-start(f32[32,40,128]{2,1,0:T(8,128)} %bitcast.3), calls=%async_computation | async-start | bytes 1310720 | tf_op jit(solution)/shard_map/all_to_all | solution.py:132
  52.8 17.5 %all-to-all-done = f32[32,40,128]{2,1,0:T(8,128)S(1)} async-done(((f32[32,40,128]{2,1,0:T(8,128)}), f32[32,40,128]{2,1,0:T(8,128)S(1)}, u32[]{:S(2)}, u32[]{:S(2)}) %all-to-all-start) | async-done | bytes 655392 | tf_op jit(solution)/shard_map/all_to_all | solution.py:132
  70.3 0.7 broadcast_in_dim.13
  71.0 3.6 %all-to-all-start.4 = ((f32[8,32,128]{2,1,0:T(8,128)}), f32[8,32,128]{2,1,0:T(8,128)S(1)}, u32[]{:S(2)}, u32[]{:S(2)}) async-start(f32[8,32,128]{2,1,0:T(8,128)} %broadcast_in_dim.13), calls=%async_computation.4 | async-start | bytes 262144 | tf_op jit(solution)/shard_map/all_to_all | solution.py:137
  74.6 0.1 reduce_sum.36
  74.6 7.9 %all-to-all-done.4 = f32[8,32,128]{2,1,0:T(8,128)S(1)} async-done(((f32[8,32,128]{2,1,0:T(8,128)}), f32[8,32,128]{2,1,0:T(8,128)S(1)}, u32[]{:S(2)}, u32[]{:S(2)}) %all-to-all-start.4) | async-done | bytes 131104 | tf_op jit(solution)/shard_map/all_to_all | solution.py:137
  82.5 0.7 broadcast_in_dim.11
  83.2 3.6 %all-to-all-start.1 = ((f32[8,40,128]{2,1,0:T(8,128)}), f32[8,40,128]{2,1,0:T(8,128)S(1)}, u32[]{:S(2)}, u32[]{:S(2)}) async-start(f32[8,40,128]{2,1,0:T(8,128)} %broadcast_in_dim.11), calls=%async_computation.1 | async-start | bytes 327680 | tf_op jit(solution)/shard_map/all_to_all | solution.py:137
  86.8 8.3 %all-to-all-done.1 = f32[8,40,128]{2,1,0:T(8,128)S(1)} async-done(((f32[8,40,128]{2,1,0:T(8,128)}), f32[8,40,128]{2,1,0:T(8,128)S(1)}, u32[]{:S(2)}, u32[]{:S(2)}) %all-to-all-start.1) | async-done | bytes 163872 | tf_op jit(solution)/shard_map/all_to_all | solution.py:137
  95.0 0.9 broadcast_in_dim.14
  95.9 4.2 %all-to-all-start.5 = ((f32[32,32,128]{2,1,0:T(8,128)}), f32[32,32,128]{2,1,0:T(8,128)S(1)}, u32[]{:S(2)}, u32[]{:S(2)}) async-start(f32[32,32,128]{2,1,0:T(8,128)} %broadcast_in_dim.14), calls=%async_computation.5 | async-start | bytes 1048576 | tf_op jit(solution)/shard_map/all_to_all | solution.py:137
  100.1 12.8 %all-to-all-done.5 = f32[32,32,128]{2,1,0:T(8,128)S(1)} async-done(((f32[32,32,128]{2,1,0:T(8,128)}), f32[32,32,128]{2,1,0:T(8,128)S(1)}, u32[]{:S(2)}, u32[]{:S(2)}) %all-to-all-start.5) | async-done | bytes 524320 | tf_op jit(solution)/shard_map/all_to_all | solution.py:137
  113.0 17.4 %all_to_all.30 = f32[32,40,128]{2,1,0:T(8,128)S(1)} all-to-all(f32[32,40,128]{2,1,0:T(8,128)S(1)} %broadcast_in_dim.12), channel_id=1, replica_groups=mesh['y'=8,'z'=8,'core'=2,'x'=4] {'z','x'}, dimensions={0} | all-to-all | bytes 1310720 | tf_op jit(solution)/shard_map/all_to_all | solution.py:137
  130.4 0.1 pad_maximum_fusion.own_ref
  130.5 0.0 copy-start.1
  130.5 9.9 %collective-permute-start.1 = (f32[2304,128]{1,0:T(8,128)S(1)}, f32[2304,128]{1,0:T(8,128)S(1)}, u32[]{:S(2)}, u32[]{:S(2)}) collective-permute-start(f32[2304,128]{1,0:T(8,128)S(1)} %pad_maximum_fusion.own_ref), channel_id=1, source_target_pairs={{0,4},{4,0},{1,5},{5,1},{2,6},{6,2},{3,7},{7,3},{8,12},{12,8},{9,1... | collective-permute-start | bytes 3538952 | tf_op jit(solution)/shard_map/ppermute | solution.py:152
  140.4 2.3 %collective-permute-done.1.other_ref = f32[2304,128]{1,0:T(8,128)S(1)} collective-permute-done((f32[2304,128]{1,0:T(8,128)S(1)}, f32[2304,128]{1,0:T(8,128)S(1)}, u32[]{:S(2)}, u32[]{:S(2)}) %collective-permute-start.1) | collective-permute-done | bytes 1179680 | tf_op jit(solution)/shard_map/ppermute | solution.py:152
  142.7 0.0 copy-start.2
  142.7 0.0 copy-done.1
  142.7 1.0 copy-done.2
  143.7 44.0 %iterate.1 = (f32[256,72]{1,0:T(8,128)}, f32[72,1024]{1,0:T(8,128)}) custom-call(s32[1]{0:T(128)} %bitcast.core_ref, f32[2304,128]{1,0:T(8,128)} %copy-done.1, f32[2304,128]{1,0:T(8,128)} %copy-done.2, f32[72,1024]{1,0:T(8,128)} %bitcast.14, f32[256,1024]{1,0:T(8,128)} %a_ref.3), custom_call_target="tpu_custom_call" | custom-call | tf_op jit(solution)/shard_map/iterate/pallas_call | solution.py:117
  187.7 1.6 copy.5
  (4 shorter events, 0.1 us)
Async XLA Ops:
  5.8 12.8 %copy-start = (f32[2,2304,128]{2,1,0:T(8,128)S(1)}, f32[2,2304,128]{2,1,0:T(8,128)}, u32[]{:S(2)}) copy-start(f32[2,2304,128]{2,1,0:T(8,128)} %local_gram.1) | copy-start | bytes 7077892
  7.3 11.2 %collective-permute-start = (f32[2304,128]{1,0:T(8,128)S(1)}, f32[2304,128]{1,0:T(8,128)S(1)}, u32[]{:S(2)}, u32[]{:S(2)}) collective-permute-start(f32[2304,128]{1,0:T(8,128)S(1)} %slice_bitcast_fusion), channel_id=1, source_target_pairs={{0,4},{4,0},{1,5},{5,1},{2,6},{6,2},{3,7},{7,3},{8,12},{12,8},{9,1... | collective-permute-start | bytes 3538952 | tf_op jit(solution)/shard_map/ppermute | solution.py:152
  19.5 20.9 %all-to-all-start.3 = ((f32[32,32,128]{2,1,0:T(8,128)}), f32[32,32,128]{2,1,0:T(8,128)S(1)}, u32[]{:S(2)}, u32[]{:S(2)}) async-start(f32[32,32,128]{2,1,0:T(8,128)} %bitcast.5), calls=%async_computation.3 | async-start | bytes 1048576 | tf_op jit(solution)/shard_map/all_to_all | solution.py:132
  40.4 29.9 %all-to-all-start = ((f32[32,40,128]{2,1,0:T(8,128)}), f32[32,40,128]{2,1,0:T(8,128)S(1)}, u32[]{:S(2)}, u32[]{:S(2)}) async-start(f32[32,40,128]{2,1,0:T(8,128)} %bitcast.3), calls=%async_computation | async-start | bytes 1310720 | tf_op jit(solution)/shard_map/all_to_all | solution.py:132
  71.0 11.5 %all-to-all-start.4 = ((f32[8,32,128]{2,1,0:T(8,128)}), f32[8,32,128]{2,1,0:T(8,128)S(1)}, u32[]{:S(2)}, u32[]{:S(2)}) async-start(f32[8,32,128]{2,1,0:T(8,128)} %broadcast_in_dim.13), calls=%async_computation.4 | async-start | bytes 262144 | tf_op jit(solution)/shard_map/all_to_all | solution.py:137
  83.2 11.8 %all-to-all-start.1 = ((f32[8,40,128]{2,1,0:T(8,128)}), f32[8,40,128]{2,1,0:T(8,128)S(1)}, u32[]{:S(2)}, u32[]{:S(2)}) async-start(f32[8,40,128]{2,1,0:T(8,128)} %broadcast_in_dim.11), calls=%async_computation.1 | async-start | bytes 327680 | tf_op jit(solution)/shard_map/all_to_all | solution.py:137
  95.9 17.0 %all-to-all-start.5 = ((f32[32,32,128]{2,1,0:T(8,128)}), f32[32,32,128]{2,1,0:T(8,128)S(1)}, u32[]{:S(2)}, u32[]{:S(2)}) async-start(f32[32,32,128]{2,1,0:T(8,128)} %broadcast_in_dim.14), calls=%async_computation.5 | async-start | bytes 1048576 | tf_op jit(solution)/shard_map/all_to_all | solution.py:137
  130.5 12.2 %copy-start.1 = (f32[2304,128]{1,0:T(8,128)}, f32[2304,128]{1,0:T(8,128)S(1)}, u32[]{:S(2)}) copy-start(f32[2304,128]{1,0:T(8,128)S(1)} %pad_maximum_fusion.own_ref) | copy-start | bytes 3538948
  130.5 12.2 %collective-permute-start.1 = (f32[2304,128]{1,0:T(8,128)S(1)}, f32[2304,128]{1,0:T(8,128)S(1)}, u32[]{:S(2)}, u32[]{:S(2)}) collective-permute-start(f32[2304,128]{1,0:T(8,128)S(1)} %pad_maximum_fusion.own_ref), channel_id=1, source_target_pairs={{0,4},{4,0},{1,5},{5,1},{2,6},{6,2},{3,7},{7,3},{8,12},{12,8},{9,1... | collective-permute-start | bytes 3538952 | tf_op jit(solution)/shard_map/ppermute | solution.py:152
  142.7 1.0 copy-start.2

commit v2 on v1

v2 whole, which is shorter than its diff:
```python
import functools
import math

import jax
import jax.numpy as jnp
from jax import lax
from jax.experimental import pallas as pl
from jax.experimental.pallas import tpu as pltpu
from jax.sharding import Mesh, PartitionSpec as P

ITERS = 2
B = 128
T = 256
AXES = ("y", "y_pair", "z", "z_pair", "core", "x")
NEAR = ("y_pair", "z_pair", "x")
FAR = ("z",), ("y",)

NT = (((1,), (1,)), ((), ()))
NN = (((1,), (0,)), ((), ()))

TILES = ((0, 3), (1, 2))
HALVES = tuple(
    tuple((i, j) for tile in tiles for j in (2 * tile, 2 * tile + 1) for i in range(j + 1))
    for tiles in TILES
)


def dot(a, b, dims=NN):
    return lax.dot_general(
        a, b, dims, precision=lax.Precision.HIGHEST, preferred_element_type=jnp.float32
    )


def part_dot(a, b):
    return lax.dot_general(a, b, NN, preferred_element_type=jnp.float32)


def split(x):
    high = x.astype(jnp.bfloat16)
    rest = x - high.astype(jnp.float32)
    mid = rest.astype(jnp.bfloat16)
    low = (rest - mid.astype(jnp.float32)).astype(jnp.bfloat16)
    return high, mid, low


def gram_kernel(half_ref, a_ref, out_ref):
    a = a_ref[...]
    rows = split(a.T)
    columns = split(a)

    def fill(half):
        for tile in TILES[half]:
            size = T * (tile + 1)
            high, mid, low = [part[:, T * tile:size] for part in columns]
            left = [part[:size, :] for part in rows]
            gram = part_dot(left[2], high) + part_dot(left[1], mid) + part_dot(left[0], low)
            gram = gram + (part_dot(left[1], high) + part_dot(left[0], mid))
            gram = gram + part_dot(left[0], high)
            for index, (i, j) in enumerate(HALVES[half]):
                if j // 2 == tile:
                    out_ref[index * B:(index + 1) * B, :] = gram[
                        i * B:(i + 1) * B, (j % 2) * B:(j % 2 + 1) * B
                    ]

    for half in range(2):
        pl.when(half_ref[0] == half)(functools.partial(fill, half))


def gram_half(half, a):
    return pl.pallas_call(
        gram_kernel,
        out_shape=jax.ShapeDtypeStruct((len(HALVES[0]) * B, B), jnp.float32),
        in_specs=[
            pl.BlockSpec(memory_space=pltpu.SMEM),
            pl.BlockSpec(memory_space=pltpu.VMEM),
        ],
        out_specs=pl.BlockSpec(memory_space=pltpu.VMEM),
        compiler_params=pltpu.CompilerParams(vmem_limit_bytes=24 * 1024 * 1024),
        cost_estimate=pl.CostEstimate(
            flops=6 * 2 * 256 * 1280 * 256, bytes_accessed=2300000, transcendentals=0
        ),
        name="gram_half",
    )(half, a)


def inverse_factor(gram, width=4):
    k = gram.shape[0]
    rows = k // 8
    wide = jnp.concatenate([gram, jnp.zeros((k, B - k), jnp.float32)], axis=1)
    tiles = [wide[8 * t:8 * t + 8, :] for t in range(rows)]
    lane = lax.broadcasted_iota(jnp.int32, (8, B), 1)
    sub = lax.broadcasted_iota(jnp.int32, (8, B), 0)

    def row_of(tile, s):
        return jnp.broadcast_to(tile[s:s + 1, :], (8, B))

    def columns(start, first):
        return [
            {u: jnp.broadcast_to(tiles[u][:, c:c + 1], (8, B)) for u in range(first, rows)}
            for c in range(start, min(start + width, k))
        ]

    scale = [None] * rows
    now = columns(0, 0)
    for start in range(0, k, width):
        t = start // 8
        ahead = columns(start + width, t)
        inside = (lane >= start) & (lane < start + width)
        for u in range(t, rows):
            if u == t:
                unit = jnp.where(lane == sub + 8 * u, 1.0, 0.0)
                tiles[u] = jnp.where(inside & (sub >= start % 8), unit, tiles[u])
            else:
                tiles[u] = jnp.where(inside, 0.0, tiles[u])
        for c in range(len(now)):
            s = start % 8 + c
            pivot = row_of(now[c][t], s)
            inverse = 1.0 / pivot
            root = lax.rsqrt(pivot)
            scale[t] = root if s == 0 else jnp.where(sub == s, root, scale[t])
            for other in now[c + 1:] + ahead:
                ratio = row_of(other[t], s) * inverse
                for u in range(t, rows):
                    other[u] = other[u] - now[c][u] * ratio
            row = row_of(tiles[t], s) * inverse
            for u in range(t, rows):
                column = jnp.where(sub > s, now[c][u], 0.0) if u == t else now[c][u]
                tiles[u] = tiles[u] - column * row
        now = ahead
    out = [jnp.where(lane <= sub + 8 * t, tiles[t], 0.0) * scale[t] for t in range(rows)]
    return jnp.concatenate(out, axis=0)[:, :k]


def times_gram(xt, parts):
    k, d = xt.shape
    p = -(-k // 16) * 16
    padded = jnp.concatenate([xt, jnp.zeros((p - k, d), jnp.float32)], axis=0)
    stack = jnp.concatenate(split(padded), axis=0)
    high = part_dot(stack, parts[0][...])
    mid = part_dot(stack[:2 * p], parts[1][...])
    low = part_dot(stack[:p], parts[2][...])
    out = (low + mid[p:] + high[2 * p:]) + (mid[:p] + high[p:2 * p]) + high[:p]
    return out[:k]


def iterate_kernel(total, core_ref, own_ref, other_ref, xt_ref, a_ref, rowt_ref, proj_ref, *parts):
    first = core_ref[0] == 0
    for half in range(2):
        for index, (i, j) in enumerate(HALVES[half]):
            where = slice(index * B, (index + 1) * B)
            mine = first if half == 0 else jnp.logical_not(first)
            block = jnp.where(mine, own_ref[where, :], other_ref[where, :])
            for part, value in zip(parts, split(block)):
                part[i * B:(i + 1) * B, j * B:(j + 1) * B] = value
            if i < j:
                for part, value in zip(parts, split(block.T)):
                    part[j * B:(j + 1) * B, i * B:(i + 1) * B] = value
    root = math.sqrt(total)
    xt = xt_ref[...]
    for step in range(ITERS + 1):
        zt = times_gram(xt, parts)
        inv = inverse_factor(dot(xt, zt, NT))
        crosst = dot(inv, zt)
        if step < ITERS:
            xt = dot(inverse_factor(dot(crosst, crosst, NT)), crosst)
    proj_ref[...] = crosst / root
    rowt_ref[...] = dot(inv, dot(xt, a_ref[...], NT)) * root


def iterate(total, core, own, other, xt, a):
    k, d = xt.shape
    vmem = pl.BlockSpec(memory_space=pltpu.VMEM)
    return pl.pallas_call(
        functools.partial(iterate_kernel, total),
        out_shape=(
            jax.ShapeDtypeStruct((k, a.shape[0]), jnp.float32),
            jax.ShapeDtypeStruct((k, d), jnp.float32),
        ),
        in_specs=[pl.BlockSpec(memory_space=pltpu.SMEM)] + [vmem] * 4,
        out_specs=(vmem, vmem),
        scratch_shapes=[pltpu.VMEM((d, d), jnp.bfloat16)] * 3,
        compiler_params=pltpu.CompilerParams(vmem_limit_bytes=32 * 1024 * 1024),
        name="iterate",
    )(core, own, other, xt, a)


def scatter_sum(v, axes):
    v = v.reshape(lax.axis_size(axes), -1, B)
    return jnp.sum(lax.all_to_all(v, axes, 0, 0, tiled=True), axis=0)


def collect(v, axes):
    copies = jnp.broadcast_to(v[None], (lax.axis_size(axes),) + v.shape)
    return lax.all_to_all(copies, axes, 0, 0, tiled=True)


def all_sum(v):
    v = scatter_sum(v, NEAR)
    for axes in FAR:
        v = jnp.sum(collect(v, axes), axis=0)
    return collect(v, NEAR).reshape(-1, B)


def swap(v):
    return lax.ppermute(v, "core", [(0, 1), (1, 0)])


def local(total, slab, test_matrix):
    core = lax.axis_index("core").astype(jnp.int32)[None]
    there = swap(gram_half(1 - core, slab))
    own = all_sum(gram_half(core, slab) + there)
    rowt, projected = iterate(total, core, own, swap(own), test_matrix.T, slab)
    return rowt.T, projected


def solution(mesh):
    fine = Mesh(mesh.devices.reshape(4, 2, 4, 2, 2, 4), AXES)
    rows = P(AXES, None)

    def run(slab, test_matrix):
        return jax.shard_map(
            functools.partial(local, slab.shape[0]),
            mesh=fine,
            in_specs=(rows, P()),
            out_specs=(rows, P()),
            check_vma=False,
        )(slab, test_matrix)

    return run
```

time: 190 us -> 114 us (0.60)
  waiting for transfers between devices: 66.9 us -> 3.14 us
  blocking collectives: 17.4 us -> 66.9 us
  starting transfers between devices: 46.7 us -> 17.3 us
  Pallas kernels: 49.1 us -> 23.5 us
  local copies, waits for them, and re-layouts: 8.12 us -> 1.35 us
    all_to_all x5 -> x0, waiting for transfers between devices: 62.2 us -> none  [the longest x2 33.2 us: scatter_sum(): return jnp.sum(lax.all_to_all(v, axes, 0, 0, tiled=True), axis=0)]
    all_to_all x1 -> x3, blocking collectives: 17.4 us -> 46.4 us  [collect(): return lax.all_to_all(copies, axes, 0, 0, tiled=True)]
    all_to_all x5 -> x0, starting transfers between devices: 28 us -> none  [the longest x2 16.7 us: scatter_sum(): return jnp.sum(lax.all_to_all(v, axes, 0, 0, tiled=True), axis=0)]
    pallas_call x1, Pallas kernels: 44 us -> 20.4 us  [iterate(): pl.pallas_call(functools.partial(iterate_kernel, total), out_shape=(jax.S...]
    all_to_all x0 -> x1, blocking collectives: none -> 20.6 us  [scatter_sum(): return jnp.sum(lax.all_to_all(v, axes, 0, 0, tiled=True), axis=0)]
    broadcast_in_dim x4 -> x3, local copies, waits for them, and re-layouts: 2.24 us -> 0.12 us  [collect(): copies = jnp.broadcast_to(v[None], (lax.axis_size(axes),) + v.shape)]
    pallas_call x1 -> x2, Pallas kernels: 5.14 us -> 3.13 us  [gram_half(): pl.pallas_call(gram_kernel, out_shape=jax.ShapeDtypeStruct((len(HALVES[0]...]
  transfers between devices with their start and end apart: 7 -> 2, of which waited for: 7 -> 2; matrix products, arithmetic and copies ran while one was open for 1% -> 0% of each run, Pallas kernels for 0% -> 1%
where the time goes in v2:
time: 114 us; the launch traced here: 113 us
  blocking collectives  66.9 us (59%)
  Pallas kernels  23.5 us (21%)
  starting transfers between devices  17.3 us (15%)
  waiting for transfers between devices  3.14 us (3%)
  local copies, waits for them, and re-layouts  1.35 us (1%)
    all_to_all x3, blocking collectives, collect(): return lax.all_to_all(copies, axes, 0, 0, tiled=True)  46.4 us
    all_to_all x1, blocking collectives, scatter_sum(): return jnp.sum(lax.all_to_all(v, axes, 0, 0, tiled=True), axis=0)  20.6 us
    pallas_call x1, Pallas kernels, iterate(): pl.pallas_call(functools.partial(iterate_kernel, total), out_shape=(jax.S...  20.4 us
    ppermute x2, starting transfers between devices, swap(): return lax.ppermute(v, 'core', [(0, 1), (1, 0)])  17.3 us
    ppermute x2, waiting for transfers between devices, swap(): return lax.ppermute(v, 'core', [(0, 1), (1, 0)])  3.14 us
    pallas_call x2, Pallas kernels, gram_half(): pl.pallas_call(gram_kernel, out_shape=jax.ShapeDtypeStruct((len(HALVES[0]...  3.13 us
  transfers between devices with their start and end apart: 2, of which 2 were waited for; matrix products, arithmetic and copies ran while one was open for 0% of the time, Pallas kernels for 1%

profile of v2, /device:TPU:1, one launch (start us, length us, event | category | flops | bytes accessed | tf_op | source)
XLA Modules:
  0.0 113.2 jit_solution(18254518923179498110)
XLA Ops:
  0.6 0.0 copy-start
  0.6 1.2 %copy-done = f32[256,1024]{1,0:T(8,128)S(1)} copy-done((f32[256,1024]{1,0:T(8,128)S(1)}, f32[256,1024]{1,0:T(8,128)}, u32[]{:S(2)}) %copy-start) | copy-done | bytes 1048600
  1.9 0.0 copy-start.1
  1.9 1.6 %gram_half.3 = f32[2304,128]{1,0:T(8,128)S(1)} custom-call(s32[1]{0:T(128)S(6)} %sub.3.half_ref, f32[256,1024]{1,0:T(8,128)S(1)} %copy-done), custom_call_target="tpu_custom_call" | custom-call | flops 1006632960 | bytes 2300000 | tf_op jit(solution)/shard_map/gram_half/pallas_call | solution.py:70
  3.4 8.8 %collective-permute-start = (f32[2304,128]{1,0:T(8,128)S(1)}, f32[2304,128]{1,0:T(8,128)S(1)}, u32[]{:S(2)}, u32[]{:S(2)}) collective-permute-start(f32[2304,128]{1,0:T(8,128)S(1)} %gram_half.3), channel_id=1, source_target_pairs={{0,4},{4,0},{1,5},{5,1},{2,6},{6,2},{3,7},{7,3},{8,12},{12,8},{9,1... | collective-permute-start | bytes 3538952 | tf_op jit(solution)/shard_map/ppermute | solution.py:205
  12.2 0.0 copy-done.1
  12.2 1.6 %gram_half.2 = f32[2304,128]{1,0:T(8,128)S(1)} custom-call(s32[1]{0:T(128)} %bitcast.half_ref.core_ref, f32[256,1024]{1,0:T(8,128)S(1)} %copy-done.1), custom_call_target="tpu_custom_call" | custom-call | flops 1006632960 | bytes 2300000 | tf_op jit(solution)/shard_map/gram_half/pallas_call | solution.py:70
  13.8 0.9 collective-permute-done
  14.7 0.1 add.3
  14.8 20.6 %all_to_all.20 = f32[16,144,128]{2,1,0:T(8,128)S(1)} all-to-all(f32[16,144,128]{2,1,0:T(8,128)S(1)} %bitcast.8), channel_id=1, replica_groups=mesh['y'=4,'y_pair'=2,'z'=4,'z_pair'=2,'core'=2,'x'=4] {'y_pair','z_pair..., dimensions={0} | all-to-all | bytes 2359296 | tf_op jit(solution)/shard_map/all_to_all | solution.py:189
  35.3 0.1 reduce_sum.27
  35.4 16.5 %all_to_all.21 = f32[4,144,128]{2,1,0:T(8,128)S(1)} all-to-all(f32[4,144,128]{2,1,0:T(8,128)S(1)} %broadcast_in_dim.9), channel_id=1, replica_groups=mesh['y'=4,'y_pair'=2,'z'=4,'z_pair'=2,'core'=2,'x'=4] {'z'}, dimensions={0} | all-to-all | bytes 589824 | tf_op jit(solution)/shard_map/all_to_all | solution.py:194
  52.0 14.4 %all_to_all.22 = f32[4,144,128]{2,1,0:T(8,128)S(1)} all-to-all(f32[4,144,128]{2,1,0:T(8,128)S(1)} %broadcast_in_dim.10), channel_id=1, replica_groups=mesh['y'=4,'y_pair'=2,'z'=4,'z_pair'=2,'core'=2,'x'=4] {'y'}, dimensions={0} | all-to-all | bytes 589824 | tf_op jit(solution)/shard_map/all_to_all | solution.py:194
  66.5 0.1 broadcast_in_dim.11
  66.6 0.0 copy-start.2
  66.6 15.4 %all_to_all.23 = f32[16,144,128]{2,1,0:T(8,128)S(1)} all-to-all(f32[16,144,128]{2,1,0:T(8,128)S(1)} %broadcast_in_dim.11), channel_id=1, replica_groups=mesh['y'=4,'y_pair'=2,'z'=4,'z_pair'=2,'core'=2,'x'=4] {'y_pair','z_pair..., dimensions={0} | all-to-all | bytes 2359296 | tf_op jit(solution)/shard_map/all_to_all | solution.py:194
  82.0 8.6 %collective-permute-start.1 = (f32[2304,128]{1,0:T(8,128)S(1)}, f32[2304,128]{1,0:T(8,128)S(1)}, u32[]{:S(2)}, u32[]{:S(2)}) collective-permute-start(f32[2304,128]{1,0:T(8,128)S(1)} %bitcast.5), channel_id=1, source_target_pairs={{0,4},{4,0},{1,5},{5,1},{2,6},{6,2},{3,7},{7,3},{8,12},{12,8},{9,1... | collective-permute-start | bytes 3538952 | tf_op jit(solution)/shard_map/ppermute | solution.py:205
  90.5 2.3 %collective-permute-done.1.other_ref = f32[2304,128]{1,0:T(8,128)S(1)} collective-permute-done((f32[2304,128]{1,0:T(8,128)S(1)}, f32[2304,128]{1,0:T(8,128)S(1)}, u32[]{:S(2)}, u32[]{:S(2)}) %collective-permute-start.1) | collective-permute-done | bytes 1179680 | tf_op jit(solution)/shard_map/ppermute | solution.py:205
  92.8 0.0 copy-done.2
  92.8 20.4 %iterate.1 = (f32[72,256]{1,0:T(8,128)}, f32[72,1024]{1,0:T(8,128)}) custom-call(s32[1]{0:T(128)} %bitcast.half_ref.core_ref, f32[2304,128]{1,0:T(8,128)S(1)} %bitcast.6, f32[2304,128]{1,0:T(8,128)S(1)} %collective-permute-done.1.other_ref, f32[72,1024]{1,0:T(8,128)S(1)} %bitcast.7, f32[256,1024]{1,0:T(8,128)S(1)} %copy-done.1), custom_call_target="tpu_custom_call" | custom-call | tf_op jit(solution)/shard_map/iterate/pallas_call | solution.py:173
  (4 shorter events, 0.1 us)
Async XLA Ops:
  0.6 1.2 %copy-start = (f32[256,1024]{1,0:T(8,128)S(1)}, f32[256,1024]{1,0:T(8,128)}, u32[]{:S(2)}) copy-start(f32[256,1024]{1,0:T(8,128)} %a_ref.5) | copy-start | bytes 3145732
  1.9 10.4 %copy-start.1 = (f32[256,1024]{1,0:T(8,128)S(1)}, f32[256,1024]{1,0:T(8,128)}, u32[]{:S(2)}) copy-start(f32[256,1024]{1,0:T(8,128)} %a_ref.5) | copy-start | bytes 3145732
  3.4 11.2 %collective-permute-start = (f32[2304,128]{1,0:T(8,128)S(1)}, f32[2304,128]{1,0:T(8,128)S(1)}, u32[]{:S(2)}, u32[]{:S(2)}) collective-permute-start(f32[2304,128]{1,0:T(8,128)S(1)} %gram_half.3), channel_id=1, source_target_pairs={{0,4},{4,0},{1,5},{5,1},{2,6},{6,2},{3,7},{7,3},{8,12},{12,8},{9,1... | collective-permute-start | bytes 3538952 | tf_op jit(solution)/shard_map/ppermute | solution.py:205
  66.6 26.3 %copy-start.2 = (f32[1024,72]{0,1:T(8,128)S(1)}, f32[1024,72]{0,1:T(8,128)}, u32[]{:S(2)}) copy-start(f32[1024,72]{0,1:T(8,128)} %param.3) | copy-start | bytes 884740
  82.0 10.8 %collective-permute-start.1 = (f32[2304,128]{1,0:T(8,128)S(1)}, f32[2304,128]{1,0:T(8,128)S(1)}, u32[]{:S(2)}, u32[]{:S(2)}) collective-permute-start(f32[2304,128]{1,0:T(8,128)S(1)} %bitcast.5), channel_id=1, source_target_pairs={{0,4},{4,0},{1,5},{5,1},{2,6},{6,2},{3,7},{7,3},{8,12},{12,8},{9,1... | collective-permute-start | bytes 3538952 | tf_op jit(solution)/shard_map/ppermute | solution.py:205

commit v3 on v2

--- a/solution.py
+++ b/solution.py
@@ -19,10 +19,14 @@
 NN = (((1,), (0,)), ((), ()))
 
 TILES = ((0, 3), (1, 2))
-HALVES = tuple(
+PAIRS = tuple(
     tuple((i, j) for tile in tiles for j in (2 * tile, 2 * tile + 1) for i in range(j + 1))
     for tiles in TILES
 )
+ABOVE = tuple(tuple(pair for pair in pairs if pair[0] < pair[1]) for pairs in PAIRS)
+DIAGONAL = tuple(tuple(pair for pair in pairs if pair[0] == pair[1]) for pairs in PAIRS)
+PACKED = len(ABOVE[0]) + len(DIAGONAL[0]) - 1
+H = B // 2
 
 
 def dot(a, b, dims=NN):
@@ -43,12 +47,24 @@
     return high, mid, low
 
 
-def gram_kernel(half_ref, a_ref, out_ref):
+def block_of(ref, index):
+    return ref[index * B:(index + 1) * B, :]
+
+
+def gram_kernel(half_ref, a_ref, *refs):
+    before, out_ref = refs if len(refs) == 2 else (None, refs[0])
     a = a_ref[...]
     rows = split(a.T)
     columns = split(a)
+    left_lanes = lax.broadcasted_iota(jnp.int32, (H, B), 1) < H
+
+    def put(index, value):
+        if before is not None:
+            value = value + block_of(before, index)
+        out_ref[index * B:(index + 1) * B, :] = value
 
     def fill(half):
+        diagonal = []
         for tile in TILES[half]:
             size = T * (tile + 1)
             high, mid, low = [part[:, T * tile:size] for part in columns]
@@ -56,31 +72,49 @@
             gram = part_dot(left[2], high) + part_dot(left[1], mid) + part_dot(left[0], low)
             gram = gram + (part_dot(left[1], high) + part_dot(left[0], mid))
             gram = gram + part_dot(left[0], high)
-            for index, (i, j) in enumerate(HALVES[half]):
+            for i, j in PAIRS[half]:
                 if j // 2 == tile:
-                    out_ref[index * B:(index + 1) * B, :] = gram[
-                        i * B:(i + 1) * B, (j % 2) * B:(j % 2 + 1) * B
-                    ]
+                    block = gram[i * B:(i + 1) * B, (j % 2) * B:(j % 2 + 1) * B]
+                    if i == j:
+                        diagonal.append(block)
+                    else:
+                        put(ABOVE[half].index((i, j)), block)
+        last = diagonal.pop()
+        guests = (last[:H], pltpu.roll(last[:H], H, 1), pltpu.roll(last[H:], H, 1))
+        for index, (block, guest) in enumerate(zip(diagonal, guests)):
+            lower = jnp.where(left_lanes, guest, block[H:])
+            put(len(ABOVE[half]) + index, jnp.concatenate([block[:H], lower], axis=0))
 
     for half in range(2):
         pl.when(half_ref[0] == half)(functools.partial(fill, half))
 
 
-def gram_half(half, a):
+def gram_half(half, a, *before):
+    vmem = pl.BlockSpec(memory_space=pltpu.VMEM)
     return pl.pallas_call(
         gram_kernel,
-        out_shape=jax.ShapeDtypeStruct((len(HALVES[0]) * B, B), jnp.float32),
-        in_specs=[
-            pl.BlockSpec(memory_space=pltpu.SMEM),
-            pl.BlockSpec(memory_space=pltpu.VMEM),
-        ],
-        out_specs=pl.BlockSpec(memory_space=pltpu.VMEM),
+        out_shape=jax.ShapeDtypeStruct((PACKED * B, B), jnp.float32),
+        in_specs=[pl.BlockSpec(memory_space=pltpu.SMEM), vmem] + [vmem] * len(before),
+        out_specs=vmem,
         compiler_params=pltpu.CompilerParams(vmem_limit_bytes=24 * 1024 * 1024),
         cost_estimate=pl.CostEstimate(
             flops=6 * 2 * 256 * 1280 * 256, bytes_accessed=2300000, transcendentals=0
         ),
         name="gram_half",
-    )(half, a)
+    )(half, a, *before)
+
+
+def unpack(half, blocks):
+    count = len(ABOVE[half])
+    low_rows = lax.broadcasted_iota(jnp.int32, (B, B), 0) >= H
+    left = lax.broadcasted_iota(jnp.int32, (B, B), 1) < H
+    guests = [block[H:] for block in blocks[count:]]
+    upper = jnp.where(left[:H], guests[0], pltpu.roll(guests[1], H, 1))
+    last = jnp.concatenate([upper, pltpu.roll(guests[2], H, 1)], axis=0)
+    for pair, block in zip(ABOVE[half], blocks):
+        yield pair, block
+    for pair, block in zip(DIAGONAL[half], list(blocks[count:]) + [last]):
+        yield pair, jnp.where(low_rows & left, block.T, block)
 
 
 def inverse_factor(gram, width=4):
@@ -103,29 +137,39 @@
     scale = [None] * rows
     now = columns(0, 0)
     for start in range(0, k, width):
-        t = start // 8
+        t, top = divmod(start, 8)
         ahead = columns(start + width, t)
         inside = (lane >= start) & (lane < start + width)
-        for u in range(t, rows):
-            if u == t:
-                unit = jnp.where(lane == sub + 8 * u, 1.0, 0.0)
-                tiles[u] = jnp.where(inside & (sub >= start % 8), unit, tiles[u])
-            else:
-                tiles[u] = jnp.where(inside, 0.0, tiles[u])
-        for c in range(len(now)):
-            s = start % 8 + c
-            pivot = row_of(now[c][t], s)
-            inverse = 1.0 / pivot
-            root = lax.rsqrt(pivot)
-            scale[t] = root if s == 0 else jnp.where(sub == s, root, scale[t])
-            for other in now[c + 1:] + ahead:
-                ratio = row_of(other[t], s) * inverse
-                for u in range(t, rows):
+        unit = jnp.where(lane == sub + 8 * t, 1.0, 0.0)
+        tiles[t] = jnp.where(inside & (sub >= top), unit, tiles[t])
+        n = len(now)
+        own = {(a, b): row_of(now[b][t], top + a) for a in range(n) for b in range(a + 1)}
+        inverse, lower = [], {}
+        for c in range(n):
+            inverse.append(1.0 / own[c, c])
+            root = lax.rsqrt(own[c, c])
+            scale[t] = root if top + c == 0 else jnp.where(sub == top + c, root, scale[t])
+            for a in range(c + 1, n):
+                lower[a, c] = own[a, c] * inverse[c]
+                for b in range(c + 1, a + 1):
+                    own[a, b] = own[a, b] - lower[a, c] * own[b, c]
+        ratios, lines = [], []
+        for c in range(n):
+            for o in range(c + 1, n):
+                now[o][t] = now[o][t] - now[c][t] * lower[o, c]
+            ratios.append([row_of(other[t], top + c) * inverse[c] for other in ahead])
+            lines.append(row_of(tiles[t], top + c) * inverse[c])
+            for other, ratio in zip(ahead, ratios[c]):
+                other[t] = other[t] - now[c][t] * ratio
+            tiles[t] = tiles[t] - jnp.where(sub > top + c, now[c][t], 0.0) * lines[c]
+        for u in range(t + 1, rows):
+            tiles[u] = jnp.where(inside, 0.0, tiles[u])
+            for c in range(n):
+                for o in range(c + 1, n):
+                    now[o][u] = now[o][u] - now[c][u] * lower[o, c]
+                for other, ratio in zip(ahead, ratios[c]):
                     other[u] = other[u] - now[c][u] * ratio
-            row = row_of(tiles[t], s) * inverse
-            for u in range(t, rows):
-                column = jnp.where(sub > s, now[c][u], 0.0) if u == t else now[c][u]
-                tiles[u] = tiles[u] - column * row
+                tiles[u] = tiles[u] - now[c][u] * lines[c]
         now = ahead
     out = [jnp.where(lane <= sub + 8 * t, tiles[t], 0.0) * scale[t] for t in range(rows)]
     return jnp.concatenate(out, axis=0)[:, :k]
@@ -143,18 +187,20 @@
     return out[:k]
 
 
+def fill_parts(half, packed, parts):
+    blocks = [block_of(packed, index) for index in range(PACKED)]
+    for (i, j), block in unpack(half, blocks):
+        for part, value in zip(parts, split(block)):
+            part[i * B:(i + 1) * B, j * B:(j + 1) * B] = value
+        if i < j:
+            for part, value in zip(parts, split(block.T)):
+                part[j * B:(j + 1) * B, i * B:(i + 1) * B] = value
+
+
 def iterate_kernel(total, core_ref, own_ref, other_ref, xt_ref, a_ref, rowt_ref, proj_ref, *parts):
     first = core_ref[0] == 0
-    for half in range(2):
-        for index, (i, j) in enumerate(HALVES[half]):
-            where = slice(index * B, (index + 1) * B)
-            mine = first if half == 0 else jnp.logical_not(first)
-            block = jnp.where(mine, own_ref[where, :], other_ref[where, :])
-            for part, value in zip(parts, split(block)):
-                part[i * B:(i + 1) * B, j * B:(j + 1) * B] = value
-            if i < j:
-                for part, value in zip(parts, split(block.T)):
-                    part[j * B:(j + 1) * B, i * B:(i + 1) * B] = value
+    fill_parts(0, jnp.where(first, own_ref[...], other_ref[...]), parts)
+    fill_parts(1, jnp.where(first, other_ref[...], own_ref[...]), parts)
     root = math.sqrt(total)
     xt = xt_ref[...]
     for step in range(ITERS + 1):
@@ -207,8 +253,8 @@
 
 def local(total, slab, test_matrix):
     core = lax.axis_index("core").astype(jnp.int32)[None]
-    there = swap(gram_half(1 - core, slab))
-    own = all_sum(gram_half(core, slab) + there)
+    there = swap(slab)
+    own = all_sum(gram_half(core, there, gram_half(core, slab)))
     rowt, projected = iterate(total, core, own, swap(own), test_matrix.T, slab)
     return rowt.T, projected
 

time: 114 us -> 112 us (0.982)
  transfers between devices with their start and end apart: 2 -> 2, of which waited for: 2 -> 1; matrix products, arithmetic and copies ran while one was open for 0% -> 0% of each run, Pallas kernels for 1% -> 1%
where the time goes in v3:
time: 112 us; the launch traced here: 111 us
  blocking collectives  66.2 us (59%)
  Pallas kernels  23.4 us (21%)
  starting transfers between devices  17.3 us (15%)
  waiting for transfers between devices  2.18 us (2%)
  local copies, waits for them, and re-layouts  1.35 us (1%)
    all_to_all x3, blocking collectives, collect(): return lax.all_to_all(copies, axes, 0, 0, tiled=True)  46 us
    all_to_all x1, blocking collectives, scatter_sum(): return jnp.sum(lax.all_to_all(v, axes, 0, 0, tiled=True), axis=0)  20.2 us
    pallas_call x1, Pallas kernels, iterate(): pl.pallas_call(functools.partial(iterate_kernel, total), out_shape=(jax.S...  20.1 us
    ppermute x2, starting transfers between devices, swap(): return lax.ppermute(v, 'core', [(0, 1), (1, 0)])  17.3 us
    pallas_call x2, Pallas kernels, gram_half(): pl.pallas_call(gram_kernel, out_shape=jax.ShapeDtypeStruct((PACKED * B, B...  3.27 us
  transfers between devices with their start and end apart: 2, of which 1 were waited for; matrix products, arithmetic and copies ran while one was open for 0% of the time, Pallas kernels for 1%

profile of v3, /device:TPU:1, one launch (start us, length us, event | category | flops | bytes accessed | tf_op | source)
XLA Modules:
  0.0 111.2 jit_solution(16492652480066776624)
XLA Ops:
  0.6 8.8 %collective-permute-start = (f32[256,1024]{1,0:T(8,128)}, f32[256,1024]{1,0:T(8,128)S(1)}, u32[]{:S(2)}, u32[]{:S(2)}) collective-permute-start(f32[256,1024]{1,0:T(8,128)} %a_ref.3), channel_id=1, source_target_pairs={{0,4},{4,0},{1,5},{5,1},{2,6},{6,2},{3,7},{7,3},{8,12},{12,8},{9,1... | collective-permute-start | bytes 3145736 | tf_op jit(solution)/shard_map/ppermute | solution.py:251
  9.4 0.0 copy-start
  9.4 1.2 %copy-done = f32[256,1024]{1,0:T(8,128)S(1)} copy-done((f32[256,1024]{1,0:T(8,128)S(1)}, f32[256,1024]{1,0:T(8,128)}, u32[]{:S(2)}) %copy-start) | copy-done | bytes 1048600
  10.7 1.6 %gram_half.2.refs_0_ = f32[2176,128]{1,0:T(8,128)S(1)} custom-call(s32[1]{0:T(128)} %bitcast.half_ref.core_ref, f32[256,1024]{1,0:T(8,128)S(1)} %copy-done), custom_call_target="tpu_custom_call" | custom-call | flops 1006632960 | bytes 2300000 | tf_op jit(solution)/shard_map/gram_half/pallas_call | solution.py:94
  12.3 0.0 collective-permute-done.a_ref
  12.3 1.6 %gram_half.3 = f32[2176,128]{1,0:T(8,128)S(1)} custom-call(s32[1]{0:T(128)} %bitcast.half_ref.core_ref, f32[256,1024]{1,0:T(8,128)S(1)} %collective-permute-done.a_ref, f32[2176,128]{1,0:T(8,128)S(1)} %gram_half.2.refs_0_), custom_call_target="tpu_custom_call" | custom-call | flops 1006632960 | bytes 2300000 | tf_op jit(solution)/shard_map/gram_half/pallas_call | solution.py:94
  14.0 20.2 %all_to_all.20 = f32[16,136,128]{2,1,0:T(8,128)S(1)} all-to-all(f32[16,136,128]{2,1,0:T(8,128)S(1)} %bitcast.7), channel_id=1, replica_groups=mesh['y'=4,'y_pair'=2,'z'=4,'z_pair'=2,'core'=2,'x'=4] {'y_pair','z_pair..., dimensions={0} | all-to-all | bytes 2228224 | tf_op jit(solution)/shard_map/all_to_all | solution.py:235
  34.2 0.1 reduce_sum.27
  34.3 16.2 %all_to_all.21 = f32[4,136,128]{2,1,0:T(8,128)S(1)} all-to-all(f32[4,136,128]{2,1,0:T(8,128)S(1)} %broadcast_in_dim.9), channel_id=1, replica_groups=mesh['y'=4,'y_pair'=2,'z'=4,'z_pair'=2,'core'=2,'x'=4] {'z'}, dimensions={0} | all-to-all | bytes 557056 | tf_op jit(solution)/shard_map/all_to_all | solution.py:240
  50.5 14.5 %all_to_all.22 = f32[4,136,128]{2,1,0:T(8,128)S(1)} all-to-all(f32[4,136,128]{2,1,0:T(8,128)S(1)} %broadcast_in_dim.10), channel_id=1, replica_groups=mesh['y'=4,'y_pair'=2,'z'=4,'z_pair'=2,'core'=2,'x'=4] {'y'}, dimensions={0} | all-to-all | bytes 557056 | tf_op jit(solution)/shard_map/all_to_all | solution.py:240
  65.0 0.1 broadcast_in_dim.11
  65.1 0.0 copy-start.1
  65.1 0.0 copy-start.2
  65.1 15.3 %all_to_all.23 = f32[16,136,128]{2,1,0:T(8,128)S(1)} all-to-all(f32[16,136,128]{2,1,0:T(8,128)S(1)} %broadcast_in_dim.11), channel_id=1, replica_groups=mesh['y'=4,'y_pair'=2,'z'=4,'z_pair'=2,'core'=2,'x'=4] {'y_pair','z_pair..., dimensions={0} | all-to-all | bytes 2228224 | tf_op jit(solution)/shard_map/all_to_all | solution.py:240
  80.4 8.5 %collective-permute-start.1 = (f32[2176,128]{1,0:T(8,128)S(1)}, f32[2176,128]{1,0:T(8,128)S(1)}, u32[]{:S(2)}, u32[]{:S(2)}) collective-permute-start(f32[2176,128]{1,0:T(8,128)S(1)} %bitcast.5), channel_id=1, source_target_pairs={{0,4},{4,0},{1,5},{5,1},{2,6},{6,2},{3,7},{7,3},{8,12},{12,8},{9,1... | collective-permute-start | bytes 3342344 | tf_op jit(solution)/shard_map/ppermute | solution.py:251
  88.9 2.2 %collective-permute-done.1.other_ref = f32[2176,128]{1,0:T(8,128)S(1)} collective-permute-done((f32[2176,128]{1,0:T(8,128)S(1)}, f32[2176,128]{1,0:T(8,128)S(1)}, u32[]{:S(2)}, u32[]{:S(2)}) %collective-permute-start.1) | collective-permute-done | bytes 1114144 | tf_op jit(solution)/shard_map/ppermute | solution.py:251
  91.1 0.0 copy-done.1
  91.1 0.0 copy-done.2
  91.1 20.1 %iterate.1 = (f32[72,256]{1,0:T(8,128)}, f32[72,1024]{1,0:T(8,128)}) custom-call(s32[1]{0:T(128)} %bitcast.half_ref.core_ref, f32[2176,128]{1,0:T(8,128)S(1)} %bitcast.6, f32[2176,128]{1,0:T(8,128)S(1)} %collective-permute-done.1.other_ref, f32[72,1024]{1,0:T(8,128)S(1)} %bitcast.8, f32[256,1024]{1,0:T(8,128)S(1)} %copy-done.1), custom_call_target="tpu_custom_call" | custom-call | tf_op jit(solution)/shard_map/iterate/pallas_call | solution.py:219
  (4 shorter events, 0.1 us)
Async XLA Ops:
  0.6 11.7 %collective-permute-start = (f32[256,1024]{1,0:T(8,128)}, f32[256,1024]{1,0:T(8,128)S(1)}, u32[]{:S(2)}, u32[]{:S(2)}) collective-permute-start(f32[256,1024]{1,0:T(8,128)} %a_ref.3), channel_id=1, source_target_pairs={{0,4},{4,0},{1,5},{5,1},{2,6},{6,2},{3,7},{7,3},{8,12},{12,8},{9,1... | collective-permute-start | bytes 3145736 | tf_op jit(solution)/shard_map/ppermute | solution.py:251
  9.4 1.2 %copy-start = (f32[256,1024]{1,0:T(8,128)S(1)}, f32[256,1024]{1,0:T(8,128)}, u32[]{:S(2)}) copy-start(f32[256,1024]{1,0:T(8,128)} %a_ref.3) | copy-start | bytes 3145732
  65.1 26.0 %copy-start.1 = (f32[256,1024]{1,0:T(8,128)S(1)}, f32[256,1024]{1,0:T(8,128)}, u32[]{:S(2)}) copy-start(f32[256,1024]{1,0:T(8,128)} %a_ref.3) | copy-start | bytes 3145732
  65.1 26.0 %copy-start.2 = (f32[1024,72]{0,1:T(8,128)S(1)}, f32[1024,72]{0,1:T(8,128)}, u32[]{:S(2)}) copy-start(f32[1024,72]{0,1:T(8,128)} %param.3) | copy-start | bytes 884740
  80.4 10.7 %collective-permute-start.1 = (f32[2176,128]{1,0:T(8,128)S(1)}, f32[2176,128]{1,0:T(8,128)S(1)}, u32[]{:S(2)}, u32[]{:S(2)}) collective-permute-start(f32[2176,128]{1,0:T(8,128)S(1)} %bitcast.5), channel_id=1, source_target_pairs={{0,4},{4,0},{1,5},{5,1},{2,6},{6,2},{3,7},{7,3},{8,12},{12,8},{9,1... | collective-permute-start | bytes 3342344 | tf_op jit(solution)/shard_map/ppermute | solution.py:251

commit v4 on v3

--- a/solution.py
+++ b/solution.py
@@ -53,9 +53,6 @@
 
 def gram_kernel(half_ref, a_ref, *refs):
     before, out_ref = refs if len(refs) == 2 else (None, refs[0])
-    a = a_ref[...]
-    rows = split(a.T)
-    columns = split(a)
     left_lanes = lax.broadcasted_iota(jnp.int32, (H, B), 1) < H
 
     def put(index, value):
@@ -64,24 +61,34 @@
         out_ref[index * B:(index + 1) * B, :] = value
 
     def fill(half):
-        diagonal = []
+        order = []
         for tile in TILES[half]:
-            size = T * (tile + 1)
-            high, mid, low = [part[:, T * tile:size] for part in columns]
-            left = [part[:size, :] for part in rows]
-            gram = part_dot(left[2], high) + part_dot(left[1], mid) + part_dot(left[0], low)
-            gram = gram + (part_dot(left[1], high) + part_dot(left[0], mid))
-            gram = gram + part_dot(left[0], high)
-            for i, j in PAIRS[half]:
-                if j // 2 == tile:
-                    block = gram[i * B:(i + 1) * B, (j % 2) * B:(j % 2 + 1) * B]
-                    if i == j:
-                        diagonal.append(block)
-                    else:
-                        put(ABOVE[half].index((i, j)), block)
-        last = diagonal.pop()
+            order += [(tile, tile)] + [(other, tile) for other in range(tile)]
+        ready, diagonal = {}, {}
+
+        def take(tile):
+            if tile not in ready:
+                value = a_ref[:, T * tile:T * (tile + 1)]
+                ready[tile] = split(value.T), split(value)
+            return ready[tile]
+
+        for row, column in order:
+            right, left = take(column)[1], take(row)[0]
+            gram = part_dot(left[2], right[0]) + part_dot(left[1], right[1])
+            gram = gram + part_dot(left[0], right[2])
+            gram = gram + (part_dot(left[1], right[0]) + part_dot(left[0], right[1]))
+            gram = gram + part_dot(left[0], right[0])
+            for r in range(2):
+                for c in range(2):
+                    pair = (2 * row + r, 2 * column + c)
+                    block = gram[r * B:(r + 1) * B, c * B:(c + 1) * B]
+                    if pair in DIAGONAL[half]:
+                        diagonal[pair] = block
+                    elif pair in ABOVE[half]:
+                        put(ABOVE[half].index(pair), block)
+        *hosts, last = [diagonal[pair] for pair in DIAGONAL[half]]
         guests = (last[:H], pltpu.roll(last[:H], H, 1), pltpu.roll(last[H:], H, 1))
-        for index, (block, guest) in enumerate(zip(diagonal, guests)):
+        for index, (block, guest) in enumerate(zip(hosts, guests)):
             lower = jnp.where(left_lanes, guest, block[H:])
             put(len(ABOVE[half]) + index, jnp.concatenate([block[:H], lower], axis=0))
 
@@ -205,12 +212,15 @@
     xt = xt_ref[...]
     for step in range(ITERS + 1):
         zt = times_gram(xt, parts)
-        inv = inverse_factor(dot(xt, zt, NT))
+        gram = dot(xt, zt, NT)
+        if step == ITERS:
+            yt = dot(xt, a_ref[...], NT)
+        inv = inverse_factor(gram)
         crosst = dot(inv, zt)
         if step < ITERS:
             xt = dot(inverse_factor(dot(crosst, crosst, NT)), crosst)
     proj_ref[...] = crosst / root
-    rowt_ref[...] = dot(inv, dot(xt, a_ref[...], NT)) * root
+    rowt_ref[...] = dot(inv, yt) * root
 
 
 def iterate(total, core, own, other, xt, a):

time: 112 us -> 109 us (0.973)
  Pallas kernels: 23.4 us -> 21.8 us
where the time goes in v4:
time: 109 us
  blocking collectives  65.4 us (60%)
  Pallas kernels  21.8 us (20%)
  starting transfers between devices  17.2 us (16%)
  waiting for transfers between devices  2.18 us (2%)
  local copies, waits for them, and re-layouts  1.35 us (1%)
    all_to_all x3, blocking collectives, collect(): return lax.all_to_all(copies, axes, 0, 0, tiled=True)  45.8 us
    all_to_all x1, blocking collectives, scatter_sum(): return jnp.sum(lax.all_to_all(v, axes, 0, 0, tiled=True), axis=0)  19.6 us
    pallas_call x1, Pallas kernels, iterate(): pl.pallas_call(functools.partial(iterate_kernel, total), out_shape=(jax.S...  19.3 us
    ppermute x2, starting transfers between devices, swap(): return lax.ppermute(v, 'core', [(0, 1), (1, 0)])  17.2 us
    pallas_call x2, Pallas kernels, gram_half(): pl.pallas_call(gram_kernel, out_shape=jax.ShapeDtypeStruct((PACKED * B, B...  2.52 us
    ppermute x2, waiting for transfers between devices, swap(): return lax.ppermute(v, 'core', [(0, 1), (1, 0)])  2.18 us
  transfers between devices with their start and end apart: 2, of which 1 were waited for; matrix products, arithmetic and copies ran while one was open for 0% of the time, Pallas kernels for 1%

profile of v4, /device:TPU:1, one launch (start us, length us, event | category | flops | bytes accessed | tf_op | source)
XLA Modules:
  0.0 108.8 jit_solution(11029692866914261343)
XLA Ops:
  0.6 8.8 %collective-permute-start = (f32[256,1024]{1,0:T(8,128)}, f32[256,1024]{1,0:T(8,128)S(1)}, u32[]{:S(2)}, u32[]{:S(2)}) collective-permute-start(f32[256,1024]{1,0:T(8,128)} %a_ref.3), channel_id=1, source_target_pairs={{0,4},{4,0},{1,5},{5,1},{2,6},{6,2},{3,7},{7,3},{8,12},{12,8},{9,1... | collective-permute-start | bytes 3145736 | tf_op jit(solution)/shard_map/ppermute | solution.py:261
  9.4 0.0 copy-start
  9.4 1.2 %copy-done = f32[256,1024]{1,0:T(8,128)S(1)} copy-done((f32[256,1024]{1,0:T(8,128)S(1)}, f32[256,1024]{1,0:T(8,128)}, u32[]{:S(2)}) %copy-start) | copy-done | bytes 1048600
  10.7 1.3 %gram_half.2.refs_0_ = f32[2176,128]{1,0:T(8,128)S(1)} custom-call(s32[1]{0:T(128)} %bitcast.half_ref.core_ref, f32[256,1024]{1,0:T(8,128)S(1)} %copy-done), custom_call_target="tpu_custom_call" | custom-call | flops 1006632960 | bytes 2300000 | tf_op jit(solution)/shard_map/gram_half/pallas_call | solution.py:101
  11.9 0.0 collective-permute-done.a_ref
  11.9 1.3 %gram_half.3 = f32[2176,128]{1,0:T(8,128)S(1)} custom-call(s32[1]{0:T(128)} %bitcast.half_ref.core_ref, f32[256,1024]{1,0:T(8,128)S(1)} %collective-permute-done.a_ref, f32[2176,128]{1,0:T(8,128)S(1)} %gram_half.2.refs_0_), custom_call_target="tpu_custom_call" | custom-call | flops 1006632960 | bytes 2300000 | tf_op jit(solution)/shard_map/gram_half/pallas_call | solution.py:101
  13.2 19.6 %all_to_all.20 = f32[16,136,128]{2,1,0:T(8,128)S(1)} all-to-all(f32[16,136,128]{2,1,0:T(8,128)S(1)} %bitcast.7), channel_id=1, replica_groups=mesh['y'=4,'y_pair'=2,'z'=4,'z_pair'=2,'core'=2,'x'=4] {'y_pair','z_pair..., dimensions={0} | all-to-all | bytes 2228224 | tf_op jit(solution)/shard_map/all_to_all | solution.py:245
  32.8 0.1 reduce_sum.27
  32.9 16.4 %all_to_all.21 = f32[4,136,128]{2,1,0:T(8,128)S(1)} all-to-all(f32[4,136,128]{2,1,0:T(8,128)S(1)} %broadcast_in_dim.9), channel_id=1, replica_groups=mesh['y'=4,'y_pair'=2,'z'=4,'z_pair'=2,'core'=2,'x'=4] {'z'}, dimensions={0} | all-to-all | bytes 557056 | tf_op jit(solution)/shard_map/all_to_all | solution.py:250
  49.4 14.5 %all_to_all.22 = f32[4,136,128]{2,1,0:T(8,128)S(1)} all-to-all(f32[4,136,128]{2,1,0:T(8,128)S(1)} %broadcast_in_dim.10), channel_id=1, replica_groups=mesh['y'=4,'y_pair'=2,'z'=4,'z_pair'=2,'core'=2,'x'=4] {'y'}, dimensions={0} | all-to-all | bytes 557056 | tf_op jit(solution)/shard_map/all_to_all | solution.py:250
  63.9 0.1 broadcast_in_dim.11
  63.9 0.0 copy-start.1
  63.9 0.0 copy-start.2
  64.0 14.9 %all_to_all.23 = f32[16,136,128]{2,1,0:T(8,128)S(1)} all-to-all(f32[16,136,128]{2,1,0:T(8,128)S(1)} %broadcast_in_dim.11), channel_id=1, replica_groups=mesh['y'=4,'y_pair'=2,'z'=4,'z_pair'=2,'core'=2,'x'=4] {'y_pair','z_pair..., dimensions={0} | all-to-all | bytes 2228224 | tf_op jit(solution)/shard_map/all_to_all | solution.py:250
  78.9 8.4 %collective-permute-start.1 = (f32[2176,128]{1,0:T(8,128)S(1)}, f32[2176,128]{1,0:T(8,128)S(1)}, u32[]{:S(2)}, u32[]{:S(2)}) collective-permute-start(f32[2176,128]{1,0:T(8,128)S(1)} %bitcast.5), channel_id=1, source_target_pairs={{0,4},{4,0},{1,5},{5,1},{2,6},{6,2},{3,7},{7,3},{8,12},{12,8},{9,1... | collective-permute-start | bytes 3342344 | tf_op jit(solution)/shard_map/ppermute | solution.py:261
  87.3 2.2 %collective-permute-done.1.other_ref = f32[2176,128]{1,0:T(8,128)S(1)} collective-permute-done((f32[2176,128]{1,0:T(8,128)S(1)}, f32[2176,128]{1,0:T(8,128)S(1)}, u32[]{:S(2)}, u32[]{:S(2)}) %collective-permute-start.1) | collective-permute-done | bytes 1114144 | tf_op jit(solution)/shard_map/ppermute | solution.py:261
  89.5 0.0 copy-done.1
  89.5 0.0 copy-done.2
  89.5 19.3 %iterate.1 = (f32[72,256]{1,0:T(8,128)}, f32[72,1024]{1,0:T(8,128)}) custom-call(s32[1]{0:T(128)} %bitcast.half_ref.core_ref, f32[2176,128]{1,0:T(8,128)S(1)} %bitcast.6, f32[2176,128]{1,0:T(8,128)S(1)} %collective-permute-done.1.other_ref, f32[72,1024]{1,0:T(8,128)S(1)} %bitcast.8, f32[256,1024]{1,0:T(8,128)S(1)} %copy-done.1), custom_call_target="tpu_custom_call" | custom-call | tf_op jit(solution)/shard_map/iterate/pallas_call | solution.py:229
  (4 shorter events, 0.1 us)
Async XLA Ops:
  0.6 11.3 %collective-permute-start = (f32[256,1024]{1,0:T(8,128)}, f32[256,1024]{1,0:T(8,128)S(1)}, u32[]{:S(2)}, u32[]{:S(2)}) collective-permute-start(f32[256,1024]{1,0:T(8,128)} %a_ref.3), channel_id=1, source_target_pairs={{0,4},{4,0},{1,5},{5,1},{2,6},{6,2},{3,7},{7,3},{8,12},{12,8},{9,1... | collective-permute-start | bytes 3145736 | tf_op jit(solution)/shard_map/ppermute | solution.py:261
  9.4 1.2 %copy-start = (f32[256,1024]{1,0:T(8,128)S(1)}, f32[256,1024]{1,0:T(8,128)}, u32[]{:S(2)}) copy-start(f32[256,1024]{1,0:T(8,128)} %a_ref.3) | copy-start | bytes 3145732
  63.9 25.6 %copy-start.1 = (f32[256,1024]{1,0:T(8,128)S(1)}, f32[256,1024]{1,0:T(8,128)}, u32[]{:S(2)}) copy-start(f32[256,1024]{1,0:T(8,128)} %a_ref.3) | copy-start | bytes 3145732
  63.9 25.6 %copy-start.2 = (f32[1024,72]{0,1:T(8,128)S(1)}, f32[1024,72]{0,1:T(8,128)}, u32[]{:S(2)}) copy-start(f32[1024,72]{0,1:T(8,128)} %param.3) | copy-start | bytes 884740
  78.9 10.6 %collective-permute-start.1 = (f32[2176,128]{1,0:T(8,128)S(1)}, f32[2176,128]{1,0:T(8,128)S(1)}, u32[]{:S(2)}, u32[]{:S(2)}) collective-permute-start(f32[2176,128]{1,0:T(8,128)S(1)} %bitcast.5), channel_id=1, source_target_pairs={{0,4},{4,0},{1,5},{5,1},{2,6},{6,2},{3,7},{7,3},{8,12},{12,8},{9,1... | collective-permute-start | bytes 3342344 | tf_op jit(solution)/shard_map/ppermute | solution.py:261

commit v5 on v4

--- a/solution.py
+++ b/solution.py
@@ -11,9 +11,27 @@
 ITERS = 2
 B = 128
 T = 256
-AXES = ("y", "y_pair", "z", "z_pair", "core", "x")
-NEAR = ("y_pair", "z_pair", "x")
-FAR = ("z",), ("y",)
+X, Y, Z = 4, 8, 8
+
+
+def device(y, z, core, x):
+    return ((y % Y * Z + z % Z) * 2 + core) * X + x % X
+
+
+NEAR = [
+    [device(y + core + a, z + core + b, core, x + core + c)
+     for a in range(2) for b in range(2) for c in range(2)]
+    for core in range(2) for y in range(0, Y, 2) for z in range(0, Z, 2) for x in range(0, X, 2)
+]
+FAR = [
+    [device(y + a, z + b, core, x + c)
+     for y in range(0, Y, 2) for z in range(0, Z, 2) for x in range(0, X, 2)]
+    for core in range(2) for a in range(2) for b in range(2) for c in range(2)
+]
+SWAP = [
+    (device(y, z, core, x), device(y, z, 1 - core, x))
+    for y in range(Y) for z in range(Z) for core in range(2) for x in range(X)
+]
 
 NT = (((1,), (1,)), ((), ()))
 NN = (((1,), (0,)), ((), ()))
@@ -240,29 +258,33 @@
     )(core, own, other, xt, a)
 
 
-def scatter_sum(v, axes):
-    v = v.reshape(lax.axis_size(axes), -1, B)
-    return jnp.sum(lax.all_to_all(v, axes, 0, 0, tiled=True), axis=0)
-
-
-def collect(v, axes):
-    copies = jnp.broadcast_to(v[None], (lax.axis_size(axes),) + v.shape)
-    return lax.all_to_all(copies, axes, 0, 0, tiled=True)
+def exchange(v, groups):
+    return lax.all_to_all(v, "device", 0, 0, axis_index_groups=groups, tiled=True)
+
+
+def scatter_sum(v, groups):
+    return jnp.sum(exchange(v.reshape(len(groups[0]), -1, B), groups), axis=0)
+
+
+def collect(v, groups):
+    copies = jnp.broadcast_to(v[None], (len(groups[0]),) + v.shape)
+    return exchange(copies, groups).reshape(-1, B)
 
 
 def all_sum(v):
     v = scatter_sum(v, NEAR)
-    for axes in FAR:
-        v = jnp.sum(collect(v, axes), axis=0)
-    return collect(v, NEAR).reshape(-1, B)
+    rows = v.shape[0]
+    v = jnp.pad(v, ((0, -rows % len(FAR[0])), (0, 0)))
+    v = collect(scatter_sum(v, FAR), FAR)[:rows]
+    return collect(v, NEAR)
 
 
 def swap(v):
-    return lax.ppermute(v, "core", [(0, 1), (1, 0)])
+    return lax.ppermute(v, "device", SWAP)
 
 
 def local(total, slab, test_matrix):
-    core = lax.axis_index("core").astype(jnp.int32)[None]
+    core = (lax.axis_index("device") // X % 2).astype(jnp.int32)[None]
     there = swap(slab)
     own = all_sum(gram_half(core, there, gram_half(core, slab)))
     rowt, projected = iterate(total, core, own, swap(own), test_matrix.T, slab)
@@ -270,13 +292,13 @@
 
 
 def solution(mesh):
-    fine = Mesh(mesh.devices.reshape(4, 2, 4, 2, 2, 4), AXES)
-    rows = P(AXES, None)
+    flat = Mesh(mesh.devices.reshape(-1), ("device",))
+    rows = P("device", None)
 
     def run(slab, test_matrix):
         return jax.shard_map(
             functools.partial(local, slab.shape[0]),
-            mesh=fine,
+            mesh=flat,
             in_specs=(rows, P()),
             out_specs=(rows, P()),
             check_vma=False,

time: 109 us -> 117 us (1.073)
  blocking collectives: 65.4 us -> 77.7 us
  starting transfers between devices: 17.2 us -> 12.8 us
    all_to_all x4, blocking collectives: 65.4 us -> 77.7 us  [exchange(): lax.all_to_all(v, 'device', 0, 0, axis_index_groups=groups, tiled=True)]
    ppermute x2, starting transfers between devices: 17.2 us -> 12.8 us  [swap(): return lax.ppermute(v, 'device', SWAP)]
where the time goes in v5:
time: 117 us
  blocking collectives  77.7 us (66%)
  Pallas kernels  21.8 us (19%)
  starting transfers between devices  12.8 us (11%)
  waiting for transfers between devices  2.18 us (2%)
  local copies, waits for them, and re-layouts  1.39 us (1%)
    all_to_all x4, blocking collectives, exchange(): lax.all_to_all(v, 'device', 0, 0, axis_index_groups=groups, tiled=True)  77.7 us
    pallas_call x1, Pallas kernels, iterate(): pl.pallas_call(functools.partial(iterate_kernel, total), out_shape=(jax.S...  19.3 us
    ppermute x2, starting transfers between devices, swap(): return lax.ppermute(v, 'device', SWAP)  12.8 us
    pallas_call x2, Pallas kernels, gram_half(): pl.pallas_call(gram_kernel, out_shape=jax.ShapeDtypeStruct((PACKED * B, B...  2.52 us
  transfers between devices with their start and end apart: 2, of which 1 were waited for; matrix products, arithmetic and copies ran while one was open for 0% of the time, Pallas kernels for 1%

profile of v5, /device:TPU:1, one launch (start us, length us, event | category | flops | bytes accessed | tf_op | source)
XLA Modules:
  0.0 116.8 jit_solution(3814793956901258684)
XLA Ops:
  0.6 8.8 %collective-permute-start = (f32[256,1024]{1,0:T(8,128)}, f32[256,1024]{1,0:T(8,128)S(1)}, u32[]{:S(2)}, u32[]{:S(2)}) collective-permute-start(f32[256,1024]{1,0:T(8,128)} %a_ref.3), channel_id=1, source_target_pairs={{0,4},{1,5},{2,6},{3,7},{4,0},{5,1},{6,2},{7,3},{8,12},{9,13},{10,... | collective-permute-start | bytes 3145736 | tf_op jit(solution)/shard_map/ppermute | solution.py:283
  9.5 0.0 copy-start
  9.5 1.2 %copy-done = f32[256,1024]{1,0:T(8,128)S(1)} copy-done((f32[256,1024]{1,0:T(8,128)S(1)}, f32[256,1024]{1,0:T(8,128)}, u32[]{:S(2)}) %copy-start) | copy-done | bytes 1048600
  10.7 1.3 %gram_half.2.refs_0_ = f32[2176,128]{1,0:T(8,128)S(1)} custom-call(s32[1]{0:T(128)} %bitcast.half_ref.core_ref, f32[256,1024]{1,0:T(8,128)S(1)} %copy-done), custom_call_target="tpu_custom_call" | custom-call | flops 1006632960 | bytes 2300000 | tf_op jit(solution)/shard_map/gram_half/pallas_call | solution.py:119
  11.9 0.0 collective-permute-done.a_ref
  12.0 1.3 %gram_half.3 = f32[2176,128]{1,0:T(8,128)S(1)} custom-call(s32[1]{0:T(128)} %bitcast.half_ref.core_ref, f32[256,1024]{1,0:T(8,128)S(1)} %collective-permute-done.a_ref, f32[2176,128]{1,0:T(8,128)S(1)} %gram_half.2.refs_0_), custom_call_target="tpu_custom_call" | custom-call | flops 1006632960 | bytes 2300000 | tf_op jit(solution)/shard_map/gram_half/pallas_call | solution.py:119
  13.2 18.3 %all_to_all.20 = f32[8,272,128]{2,1,0:T(8,128)S(1)} all-to-all(f32[8,272,128]{2,1,0:T(8,128)S(1)} %bitcast.7), channel_id=1, replica_groups={{0,1,8,9,64,65,72,73},{2,3,10,11,66,67,74,75},{16,17,24,25,80,81,88,89}..., dimensions={0} | all-to-all | bytes 2228224 | tf_op jit(solution)/shard_map/all_to_all | solution.py:262
  31.5 0.1 reduce_sum.18
  31.6 24.6 %all_to_all.21 = f32[32,9,128]{2,1,0:T(8,128)S(1)} all-to-all(f32[32,9,128]{2,1,0:T(8,128)S(1)} %reshape.19), channel_id=1, replica_groups={{0,2,16,18,32,34,48,50,128,130,144,146,160,162,176,178,256,258,272,274,..., dimensions={0} | all-to-all | bytes 294912 | tf_op jit(solution)/shard_map/all_to_all | solution.py:262
  56.3 19.2 %all_to_all.22 = f32[32,9,128]{2,1,0:T(8,128)S(1)} all-to-all(f32[32,9,128]{2,1,0:T(8,128)S(1)} %broadcast_in_dim.7), channel_id=1, replica_groups={{0,2,16,18,32,34,48,50,128,130,144,146,160,162,176,178,256,258,272,274,..., dimensions={0} | all-to-all | bytes 294912 | tf_op jit(solution)/shard_map/all_to_all | solution.py:262
  75.6 0.1 broadcast_in_dim.8
  75.7 0.0 copy-start.1
  75.7 0.0 copy-start.2
  75.7 15.6 %all_to_all.23 = f32[8,272,128]{2,1,0:T(8,128)S(1)} all-to-all(f32[8,272,128]{2,1,0:T(8,128)S(1)} %broadcast_in_dim.8), channel_id=1, replica_groups={{0,1,8,9,64,65,72,73},{2,3,10,11,66,67,74,75},{16,17,24,25,80,81,88,89}..., dimensions={0} | all-to-all | bytes 2228224 | tf_op jit(solution)/shard_map/all_to_all | solution.py:262
  91.3 4.0 %collective-permute-start.1 = (f32[2176,128]{1,0:T(8,128)S(1)}, f32[2176,128]{1,0:T(8,128)S(1)}, u32[]{:S(2)}, u32[]{:S(2)}) collective-permute-start(f32[2176,128]{1,0:T(8,128)S(1)} %bitcast.5), channel_id=1, source_target_pairs={{0,4},{1,5},{2,6},{3,7},{4,0},{5,1},{6,2},{7,3},{8,12},{9,13},{10,... | collective-permute-start | bytes 3342344 | tf_op jit(solution)/shard_map/ppermute | solution.py:283
  95.3 2.2 %collective-permute-done.1.other_ref = f32[2176,128]{1,0:T(8,128)S(1)} collective-permute-done((f32[2176,128]{1,0:T(8,128)S(1)}, f32[2176,128]{1,0:T(8,128)S(1)}, u32[]{:S(2)}, u32[]{:S(2)}) %collective-permute-start.1) | collective-permute-done | bytes 1114144 | tf_op jit(solution)/shard_map/ppermute | solution.py:283
  97.5 0.0 copy-done.1
  97.5 0.0 copy-done.2
  97.5 19.3 %iterate.1 = (f32[72,256]{1,0:T(8,128)}, f32[72,1024]{1,0:T(8,128)}) custom-call(s32[1]{0:T(128)} %bitcast.half_ref.core_ref, f32[2176,128]{1,0:T(8,128)S(1)} %bitcast.6, f32[2176,128]{1,0:T(8,128)S(1)} %collective-permute-done.1.other_ref, f32[72,1024]{1,0:T(8,128)S(1)} %bitcast.8, f32[256,1024]{1,0:T(8,128)S(1)} %copy-done.1), custom_call_target="tpu_custom_call" | custom-call | tf_op jit(solution)/shard_map/iterate/pallas_call | solution.py:247
  (6 shorter events, 0.1 us)
Async XLA Ops:
  0.6 11.3 %collective-permute-start = (f32[256,1024]{1,0:T(8,128)}, f32[256,1024]{1,0:T(8,128)S(1)}, u32[]{:S(2)}, u32[]{:S(2)}) collective-permute-start(f32[256,1024]{1,0:T(8,128)} %a_ref.3), channel_id=1, source_target_pairs={{0,4},{1,5},{2,6},{3,7},{4,0},{5,1},{6,2},{7,3},{8,12},{9,13},{10,... | collective-permute-start | bytes 3145736 | tf_op jit(solution)/shard_map/ppermute | solution.py:283
  9.5 1.2 %copy-start = (f32[256,1024]{1,0:T(8,128)S(1)}, f32[256,1024]{1,0:T(8,128)}, u32[]{:S(2)}) copy-start(f32[256,1024]{1,0:T(8,128)} %a_ref.3) | copy-start | bytes 3145732
  75.7 21.8 %copy-start.1 = (f32[256,1024]{1,0:T(8,128)S(1)}, f32[256,1024]{1,0:T(8,128)}, u32[]{:S(2)}) copy-start(f32[256,1024]{1,0:T(8,128)} %a_ref.3) | copy-start | bytes 3145732
  75.7 21.8 %copy-start.2 = (f32[1024,72]{0,1:T(8,128)S(1)}, f32[1024,72]{0,1:T(8,128)}, u32[]{:S(2)}) copy-start(f32[1024,72]{0,1:T(8,128)} %param.3) | copy-start | bytes 884740
  91.3 6.2 %collective-permute-start.1 = (f32[2176,128]{1,0:T(8,128)S(1)}, f32[2176,128]{1,0:T(8,128)S(1)}, u32[]{:S(2)}, u32[]{:S(2)}) collective-permute-start(f32[2176,128]{1,0:T(8,128)S(1)} %bitcast.5), channel_id=1, source_target_pairs={{0,4},{1,5},{2,6},{3,7},{4,0},{5,1},{6,2},{7,3},{8,12},{9,13},{10,... | collective-permute-start | bytes 3342344 | tf_op jit(solution)/shard_map/ppermute | solution.py:283

commit v6 on v5

--- a/solution.py
+++ b/solution.py
@@ -19,15 +19,20 @@
 
 
 NEAR = [
-    [device(y + core + a, z + core + b, core, x + core + c)
-     for a in range(2) for b in range(2) for c in range(2)]
-    for core in range(2) for y in range(0, Y, 2) for z in range(0, Z, 2) for x in range(0, X, 2)
+    [device(y + core + a, z + core + b, core, x)
+     for a in range(2) for b in range(2) for x in range(X)]
+    for core in range(2) for y in range(0, Y, 2) for z in range(0, Z, 2)
 ]
-FAR = [
-    [device(y + a, z + b, core, x + c)
-     for y in range(0, Y, 2) for z in range(0, Z, 2) for x in range(0, X, 2)]
-    for core in range(2) for a in range(2) for b in range(2) for c in range(2)
-]
+FAR = (
+    [
+        [device(y, z + a, core, x) for z in range(0, Z, 2)]
+        for y in range(Y) for core in range(2) for x in range(X) for a in range(2)
+    ],
+    [
+        [device(y + a, z, core, x) for y in range(0, Y, 2)]
+        for z in range(Z) for core in range(2) for x in range(X) for a in range(2)
+    ],
+)
 SWAP = [
     (device(y, z, core, x), device(y, z, 1 - core, x))
     for y in range(Y) for z in range(Z) for core in range(2) for x in range(X)
@@ -268,15 +273,14 @@
 
 def collect(v, groups):
     copies = jnp.broadcast_to(v[None], (len(groups[0]),) + v.shape)
-    return exchange(copies, groups).reshape(-1, B)
+    return exchange(copies, groups)
 
 
 def all_sum(v):
     v = scatter_sum(v, NEAR)
-    rows = v.shape[0]
-    v = jnp.pad(v, ((0, -rows % len(FAR[0])), (0, 0)))
-    v = collect(scatter_sum(v, FAR), FAR)[:rows]
-    return collect(v, NEAR)
+    for groups in FAR:
+        v = jnp.sum(collect(v, groups), axis=0)
+    return collect(v, NEAR).reshape(-1, B)
 
 
 def swap(v):

time: 117 us -> 114 us (0.974)
  starting transfers between devices: 12.8 us -> 11.1 us
  blocking collectives: 77.7 us -> 76.1 us
    ppermute x2, starting transfers between devices: 12.8 us -> 11.1 us  [swap(): return lax.ppermute(v, 'device', SWAP)]
    all_to_all x4, blocking collectives: 77.7 us -> 76.1 us  [exchange(): lax.all_to_all(v, 'device', 0, 0, axis_index_groups=groups, tiled=True)]
where the time goes in v6:
time: 114 us
  blocking collectives  76.1 us (67%)
  Pallas kernels  21.8 us (19%)
  starting transfers between devices  11.1 us (10%)
  waiting for transfers between devices  2.37 us (2%)
  local copies, waits for them, and re-layouts  1.35 us (1%)
    all_to_all x4, blocking collectives, exchange(): lax.all_to_all(v, 'device', 0, 0, axis_index_groups=groups, tiled=True)  76.1 us
    pallas_call x1, Pallas kernels, iterate(): pl.pallas_call(functools.partial(iterate_kernel, total), out_shape=(jax.S...  19.3 us
    ppermute x2, starting transfers between devices, swap(): return lax.ppermute(v, 'device', SWAP)  11.1 us
    pallas_call x2, Pallas kernels, gram_half(): pl.pallas_call(gram_kernel, out_shape=jax.ShapeDtypeStruct((PACKED * B, B...  2.52 us
    ppermute x2, waiting for transfers between devices, swap(): return lax.ppermute(v, 'device', SWAP)  2.37 us
  transfers between devices with their start and end apart: 2, of which 1 were waited for; matrix products, arithmetic and copies ran while one was open for 0% of the time, Pallas kernels for 1%

profile of v6, /device:TPU:1, one launch (start us, length us, event | category | flops | bytes accessed | tf_op | source)
XLA Modules:
  0.0 113.6 jit_solution(4239505932316664963)
XLA Ops:
  0.6 8.8 %collective-permute-start = (f32[256,1024]{1,0:T(8,128)}, f32[256,1024]{1,0:T(8,128)S(1)}, u32[]{:S(2)}, u32[]{:S(2)}) collective-permute-start(f32[256,1024]{1,0:T(8,128)} %a_ref.3), channel_id=1, source_target_pairs={{0,4},{1,5},{2,6},{3,7},{4,0},{5,1},{6,2},{7,3},{8,12},{9,13},{10,... | collective-permute-start | bytes 3145736 | tf_op jit(solution)/shard_map/ppermute | solution.py:287
  9.5 0.0 copy-start
  9.5 1.2 %copy-done = f32[256,1024]{1,0:T(8,128)S(1)} copy-done((f32[256,1024]{1,0:T(8,128)S(1)}, f32[256,1024]{1,0:T(8,128)}, u32[]{:S(2)}) %copy-start) | copy-done | bytes 1048600
  10.7 1.3 %gram_half.2.refs_0_ = f32[2176,128]{1,0:T(8,128)S(1)} custom-call(s32[1]{0:T(128)} %bitcast.half_ref.core_ref, f32[256,1024]{1,0:T(8,128)S(1)} %copy-done), custom_call_target="tpu_custom_call" | custom-call | flops 1006632960 | bytes 2300000 | tf_op jit(solution)/shard_map/gram_half/pallas_call | solution.py:124
  11.9 0.0 collective-permute-done.a_ref
  12.0 1.3 %gram_half.3 = f32[2176,128]{1,0:T(8,128)S(1)} custom-call(s32[1]{0:T(128)} %bitcast.half_ref.core_ref, f32[256,1024]{1,0:T(8,128)S(1)} %collective-permute-done.a_ref, f32[2176,128]{1,0:T(8,128)S(1)} %gram_half.2.refs_0_), custom_call_target="tpu_custom_call" | custom-call | flops 1006632960 | bytes 2300000 | tf_op jit(solution)/shard_map/gram_half/pallas_call | solution.py:124
  13.2 20.5 %all_to_all.20 = f32[16,136,128]{2,1,0:T(8,128)S(1)} all-to-all(f32[16,136,128]{2,1,0:T(8,128)S(1)} %bitcast.7), channel_id=1, replica_groups={{0,1,2,3,8,9,10,11,64,65,66,67,72,73,74,75},{16,17,18,19,24,25,26,27,80..., dimensions={0} | all-to-all | bytes 2228224 | tf_op jit(solution)/shard_map/all_to_all | solution.py:267
  33.7 0.1 reduce_sum.27
  33.8 18.5 %all_to_all.21 = f32[4,136,128]{2,1,0:T(8,128)S(1)} all-to-all(f32[4,136,128]{2,1,0:T(8,128)S(1)} %broadcast_in_dim.9), channel_id=1, replica_groups={{0,16,32,48},{8,24,40,56},{1,17,33,49},{9,25,41,57},{2,18,34,50},{10,26..., dimensions={0} | all-to-all | bytes 557056 | tf_op jit(solution)/shard_map/all_to_all | solution.py:267
  52.4 14.4 %all_to_all.22 = f32[4,136,128]{2,1,0:T(8,128)S(1)} all-to-all(f32[4,136,128]{2,1,0:T(8,128)S(1)} %broadcast_in_dim.10), channel_id=1, replica_groups={{0,128,256,384},{64,192,320,448},{1,129,257,385},{65,193,321,449},{2,13..., dimensions={0} | all-to-all | bytes 557056 | tf_op jit(solution)/shard_map/all_to_all | solution.py:267
  66.8 0.1 broadcast_in_dim.11
  66.8 0.0 copy-start.1
  66.9 0.0 copy-start.2
  66.9 22.8 %all_to_all.23 = f32[16,136,128]{2,1,0:T(8,128)S(1)} all-to-all(f32[16,136,128]{2,1,0:T(8,128)S(1)} %broadcast_in_dim.11), channel_id=1, replica_groups={{0,1,2,3,8,9,10,11,64,65,66,67,72,73,74,75},{16,17,18,19,24,25,26,27,80..., dimensions={0} | all-to-all | bytes 2228224 | tf_op jit(solution)/shard_map/all_to_all | solution.py:267
  89.6 2.3 %collective-permute-start.1 = (f32[2176,128]{1,0:T(8,128)S(1)}, f32[2176,128]{1,0:T(8,128)S(1)}, u32[]{:S(2)}, u32[]{:S(2)}) collective-permute-start(f32[2176,128]{1,0:T(8,128)S(1)} %bitcast.5), channel_id=1, source_target_pairs={{0,4},{1,5},{2,6},{3,7},{4,0},{5,1},{6,2},{7,3},{8,12},{9,13},{10,... | collective-permute-start | bytes 3342344 | tf_op jit(solution)/shard_map/ppermute | solution.py:287
  91.9 2.4 %collective-permute-done.1.other_ref = f32[2176,128]{1,0:T(8,128)S(1)} collective-permute-done((f32[2176,128]{1,0:T(8,128)S(1)}, f32[2176,128]{1,0:T(8,128)S(1)}, u32[]{:S(2)}, u32[]{:S(2)}) %collective-permute-start.1) | collective-permute-done | bytes 1114144 | tf_op jit(solution)/shard_map/ppermute | solution.py:287
  94.3 0.0 copy-done.1
  94.3 0.0 copy-done.2
  94.3 19.3 %iterate.1 = (f32[72,256]{1,0:T(8,128)}, f32[72,1024]{1,0:T(8,128)}) custom-call(s32[1]{0:T(128)} %bitcast.half_ref.core_ref, f32[2176,128]{1,0:T(8,128)S(1)} %bitcast.6, f32[2176,128]{1,0:T(8,128)S(1)} %collective-permute-done.1.other_ref, f32[72,1024]{1,0:T(8,128)S(1)} %bitcast.8, f32[256,1024]{1,0:T(8,128)S(1)} %copy-done.1), custom_call_target="tpu_custom_call" | custom-call | tf_op jit(solution)/shard_map/iterate/pallas_call | solution.py:252
  (4 shorter events, 0.1 us)
Async XLA Ops:
  0.6 11.3 %collective-permute-start = (f32[256,1024]{1,0:T(8,128)}, f32[256,1024]{1,0:T(8,128)S(1)}, u32[]{:S(2)}, u32[]{:S(2)}) collective-permute-start(f32[256,1024]{1,0:T(8,128)} %a_ref.3), channel_id=1, source_target_pairs={{0,4},{1,5},{2,6},{3,7},{4,0},{5,1},{6,2},{7,3},{8,12},{9,13},{10,... | collective-permute-start | bytes 3145736 | tf_op jit(solution)/shard_map/ppermute | solution.py:287
  9.5 1.2 %copy-start = (f32[256,1024]{1,0:T(8,128)S(1)}, f32[256,1024]{1,0:T(8,128)}, u32[]{:S(2)}) copy-start(f32[256,1024]{1,0:T(8,128)} %a_ref.3) | copy-start | bytes 3145732
  66.8 27.4 %copy-start.1 = (f32[256,1024]{1,0:T(8,128)S(1)}, f32[256,1024]{1,0:T(8,128)}, u32[]{:S(2)}) copy-start(f32[256,1024]{1,0:T(8,128)} %a_ref.3) | copy-start | bytes 3145732
  66.9 27.4 %copy-start.2 = (f32[1024,72]{0,1:T(8,128)S(1)}, f32[1024,72]{0,1:T(8,128)}, u32[]{:S(2)}) copy-start(f32[1024,72]{0,1:T(8,128)} %param.3) | copy-start | bytes 884740
  89.6 4.6 %collective-permute-start.1 = (f32[2176,128]{1,0:T(8,128)S(1)}, f32[2176,128]{1,0:T(8,128)S(1)}, u32[]{:S(2)}, u32[]{:S(2)}) collective-permute-start(f32[2176,128]{1,0:T(8,128)S(1)} %bitcast.5), channel_id=1, source_target_pairs={{0,4},{1,5},{2,6},{3,7},{4,0},{5,1},{6,2},{7,3},{8,12},{9,13},{10,... | collective-permute-start | bytes 3342344 | tf_op jit(solution)/shard_map/ppermute | solution.py:287

commit v7 on v4

--- a/solution.py
+++ b/solution.py
@@ -210,15 +210,21 @@
     fill_parts(1, jnp.where(first, other_ref[...], own_ref[...]), parts)
     root = math.sqrt(total)
     xt = xt_ref[...]
+    zt = times_gram(xt, parts)
     for step in range(ITERS + 1):
-        zt = times_gram(xt, parts)
         gram = dot(xt, zt, NT)
         if step == ITERS:
             yt = dot(xt, a_ref[...], NT)
         inv = inverse_factor(gram)
         crosst = dot(inv, zt)
-        if step < ITERS:
-            xt = dot(inverse_factor(dot(crosst, crosst, NT)), crosst)
+        if step == ITERS:
+            break
+        square = dot(crosst, crosst, NT)
+        if step == 0:
+            ahead = times_gram(crosst, parts)
+        inv = inverse_factor(square)
+        xt = dot(inv, crosst)
+        zt = dot(inv, ahead) if step == 0 else times_gram(xt, parts)
     proj_ref[...] = crosst / root
     rowt_ref[...] = dot(inv, yt) * root
 

time: 109 us -> 108 us (level)
  no operation moved by 1% of the time
where the time goes in v7:
time: 108 us
  blocking collectives  65.4 us (61%)
  Pallas kernels  21.1 us (20%)
  starting transfers between devices  17.2 us (16%)
  waiting for transfers between devices  2.18 us (2%)
  local copies, waits for them, and re-layouts  1.35 us (1%)
    all_to_all x3, blocking collectives, collect(): return lax.all_to_all(copies, axes, 0, 0, tiled=True)  45.8 us
    all_to_all x1, blocking collectives, scatter_sum(): return jnp.sum(lax.all_to_all(v, axes, 0, 0, tiled=True), axis=0)  19.6 us
    pallas_call x1, Pallas kernels, iterate(): pl.pallas_call(functools.partial(iterate_kernel, total), out_shape=(jax.S...  18.6 us
    ppermute x2, starting transfers between devices, swap(): return lax.ppermute(v, 'core', [(0, 1), (1, 0)])  17.2 us
    pallas_call x2, Pallas kernels, gram_half(): pl.pallas_call(gram_kernel, out_shape=jax.ShapeDtypeStruct((PACKED * B, B...  2.52 us
    ppermute x2, waiting for transfers between devices, swap(): return lax.ppermute(v, 'core', [(0, 1), (1, 0)])  2.18 us
  transfers between devices with their start and end apart: 2, of which 1 were waited for; matrix products, arithmetic and copies ran while one was open for 0% of the time, Pallas kernels for 1%

profile of v7, /device:TPU:1, one launch (start us, length us, event | category | flops | bytes accessed | tf_op | source)
XLA Modules:
  0.0 108.1 jit_solution(10502057456525062555)
XLA Ops:
  0.6 8.8 %collective-permute-start = (f32[256,1024]{1,0:T(8,128)}, f32[256,1024]{1,0:T(8,128)S(1)}, u32[]{:S(2)}, u32[]{:S(2)}) collective-permute-start(f32[256,1024]{1,0:T(8,128)} %a_ref.3), channel_id=1, source_target_pairs={{0,4},{4,0},{1,5},{5,1},{2,6},{6,2},{3,7},{7,3},{8,12},{12,8},{9,1... | collective-permute-start | bytes 3145736 | tf_op jit(solution)/shard_map/ppermute | solution.py:267
  9.4 0.0 copy-start
  9.4 1.2 %copy-done = f32[256,1024]{1,0:T(8,128)S(1)} copy-done((f32[256,1024]{1,0:T(8,128)S(1)}, f32[256,1024]{1,0:T(8,128)}, u32[]{:S(2)}) %copy-start) | copy-done | bytes 1048600
  10.7 1.3 %gram_half.2.refs_0_ = f32[2176,128]{1,0:T(8,128)S(1)} custom-call(s32[1]{0:T(128)} %bitcast.half_ref.core_ref, f32[256,1024]{1,0:T(8,128)S(1)} %copy-done), custom_call_target="tpu_custom_call" | custom-call | flops 1006632960 | bytes 2300000 | tf_op jit(solution)/shard_map/gram_half/pallas_call | solution.py:101
  11.9 0.0 collective-permute-done.a_ref
  11.9 1.3 %gram_half.3 = f32[2176,128]{1,0:T(8,128)S(1)} custom-call(s32[1]{0:T(128)} %bitcast.half_ref.core_ref, f32[256,1024]{1,0:T(8,128)S(1)} %collective-permute-done.a_ref, f32[2176,128]{1,0:T(8,128)S(1)} %gram_half.2.refs_0_), custom_call_target="tpu_custom_call" | custom-call | flops 1006632960 | bytes 2300000 | tf_op jit(solution)/shard_map/gram_half/pallas_call | solution.py:101
  13.2 19.6 %all_to_all.20 = f32[16,136,128]{2,1,0:T(8,128)S(1)} all-to-all(f32[16,136,128]{2,1,0:T(8,128)S(1)} %bitcast.7), channel_id=1, replica_groups=mesh['y'=4,'y_pair'=2,'z'=4,'z_pair'=2,'core'=2,'x'=4] {'y_pair','z_pair..., dimensions={0} | all-to-all | bytes 2228224 | tf_op jit(solution)/shard_map/all_to_all | solution.py:251
  32.8 0.1 reduce_sum.27
  32.9 16.4 %all_to_all.21 = f32[4,136,128]{2,1,0:T(8,128)S(1)} all-to-all(f32[4,136,128]{2,1,0:T(8,128)S(1)} %broadcast_in_dim.9), channel_id=1, replica_groups=mesh['y'=4,'y_pair'=2,'z'=4,'z_pair'=2,'core'=2,'x'=4] {'z'}, dimensions={0} | all-to-all | bytes 557056 | tf_op jit(solution)/shard_map/all_to_all | solution.py:256
  49.4 14.5 %all_to_all.22 = f32[4,136,128]{2,1,0:T(8,128)S(1)} all-to-all(f32[4,136,128]{2,1,0:T(8,128)S(1)} %broadcast_in_dim.10), channel_id=1, replica_groups=mesh['y'=4,'y_pair'=2,'z'=4,'z_pair'=2,'core'=2,'x'=4] {'y'}, dimensions={0} | all-to-all | bytes 557056 | tf_op jit(solution)/shard_map/all_to_all | solution.py:256
  63.9 0.1 broadcast_in_dim.11
  63.9 0.0 copy-start.1
  63.9 0.0 copy-start.2
  64.0 14.9 %all_to_all.23 = f32[16,136,128]{2,1,0:T(8,128)S(1)} all-to-all(f32[16,136,128]{2,1,0:T(8,128)S(1)} %broadcast_in_dim.11), channel_id=1, replica_groups=mesh['y'=4,'y_pair'=2,'z'=4,'z_pair'=2,'core'=2,'x'=4] {'y_pair','z_pair..., dimensions={0} | all-to-all | bytes 2228224 | tf_op jit(solution)/shard_map/all_to_all | solution.py:256
  78.9 8.4 %collective-permute-start.1 = (f32[2176,128]{1,0:T(8,128)S(1)}, f32[2176,128]{1,0:T(8,128)S(1)}, u32[]{:S(2)}, u32[]{:S(2)}) collective-permute-start(f32[2176,128]{1,0:T(8,128)S(1)} %bitcast.5), channel_id=1, source_target_pairs={{0,4},{4,0},{1,5},{5,1},{2,6},{6,2},{3,7},{7,3},{8,12},{12,8},{9,1... | collective-permute-start | bytes 3342344 | tf_op jit(solution)/shard_map/ppermute | solution.py:267
  87.3 2.2 %collective-permute-done.1.other_ref = f32[2176,128]{1,0:T(8,128)S(1)} collective-permute-done((f32[2176,128]{1,0:T(8,128)S(1)}, f32[2176,128]{1,0:T(8,128)S(1)}, u32[]{:S(2)}, u32[]{:S(2)}) %collective-permute-start.1) | collective-permute-done | bytes 1114144 | tf_op jit(solution)/shard_map/ppermute | solution.py:267
  89.5 0.0 copy-done.1
  89.5 0.0 copy-done.2
  89.5 18.6 %iterate.1 = (f32[72,256]{1,0:T(8,128)}, f32[72,1024]{1,0:T(8,128)}) custom-call(s32[1]{0:T(128)} %bitcast.half_ref.core_ref, f32[2176,128]{1,0:T(8,128)S(1)} %bitcast.6, f32[2176,128]{1,0:T(8,128)S(1)} %collective-permute-done.1.other_ref, f32[72,1024]{1,0:T(8,128)S(1)} %bitcast.8, f32[256,1024]{1,0:T(8,128)S(1)} %copy-done.1), custom_call_target="tpu_custom_call" | custom-call | tf_op jit(solution)/shard_map/iterate/pallas_call | solution.py:235
  (4 shorter events, 0.1 us)
Async XLA Ops:
  0.6 11.3 %collective-permute-start = (f32[256,1024]{1,0:T(8,128)}, f32[256,1024]{1,0:T(8,128)S(1)}, u32[]{:S(2)}, u32[]{:S(2)}) collective-permute-start(f32[256,1024]{1,0:T(8,128)} %a_ref.3), channel_id=1, source_target_pairs={{0,4},{4,0},{1,5},{5,1},{2,6},{6,2},{3,7},{7,3},{8,12},{12,8},{9,1... | collective-permute-start | bytes 3145736 | tf_op jit(solution)/shard_map/ppermute | solution.py:267
  9.4 1.2 %copy-start = (f32[256,1024]{1,0:T(8,128)S(1)}, f32[256,1024]{1,0:T(8,128)}, u32[]{:S(2)}) copy-start(f32[256,1024]{1,0:T(8,128)} %a_ref.3) | copy-start | bytes 3145732
  63.9 25.6 %copy-start.1 = (f32[256,1024]{1,0:T(8,128)S(1)}, f32[256,1024]{1,0:T(8,128)}, u32[]{:S(2)}) copy-start(f32[256,1024]{1,0:T(8,128)} %a_ref.3) | copy-start | bytes 3145732
  63.9 25.6 %copy-start.2 = (f32[1024,72]{0,1:T(8,128)S(1)}, f32[1024,72]{0,1:T(8,128)}, u32[]{:S(2)}) copy-start(f32[1024,72]{0,1:T(8,128)} %param.3) | copy-start | bytes 884740
  78.9 10.6 %collective-permute-start.1 = (f32[2176,128]{1,0:T(8,128)S(1)}, f32[2176,128]{1,0:T(8,128)S(1)}, u32[]{:S(2)}, u32[]{:S(2)}) collective-permute-start(f32[2176,128]{1,0:T(8,128)S(1)} %bitcast.5), channel_id=1, source_target_pairs={{0,4},{4,0},{1,5},{5,1},{2,6},{6,2},{3,7},{7,3},{8,12},{12,8},{9,1... | collective-permute-start | bytes 3342344 | tf_op jit(solution)/shard_map/ppermute | solution.py:267

commit v8 on v6

--- a/solution.py
+++ b/solution.py
@@ -19,20 +19,26 @@
 
 
 NEAR = [
-    [device(y + core + a, z + core + b, core, x)
-     for a in range(2) for b in range(2) for x in range(X)]
+    [device(y + a, z + b, core, x) for a in range(2) for b in range(2) for x in range(X)]
     for core in range(2) for y in range(0, Y, 2) for z in range(0, Z, 2)
 ]
-FAR = (
-    [
+
+
+def along_z(core):
+    return [
         [device(y, z + a, core, x) for z in range(0, Z, 2)]
-        for y in range(Y) for core in range(2) for x in range(X) for a in range(2)
-    ],
-    [
+        for y in range(Y) for x in range(X) for a in range(2)
+    ]
+
+
+def along_y(core):
+    return [
         [device(y + a, z, core, x) for y in range(0, Y, 2)]
-        for z in range(Z) for core in range(2) for x in range(X) for a in range(2)
-    ],
-)
+        for z in range(Z) for x in range(X) for a in range(2)
+    ]
+
+
+FAR = along_z(0) + along_y(1), along_y(0) + along_z(1)
 SWAP = [
     (device(y, z, core, x), device(y, z, 1 - core, x))
     for y in range(Y) for z in range(Z) for core in range(2) for x in range(X)
@@ -233,15 +239,21 @@
     fill_parts(1, jnp.where(first, other_ref[...], own_ref[...]), parts)
     root = math.sqrt(total)
     xt = xt_ref[...]
+    zt = times_gram(xt, parts)
     for step in range(ITERS + 1):
-        zt = times_gram(xt, parts)
         gram = dot(xt, zt, NT)
         if step == ITERS:
             yt = dot(xt, a_ref[...], NT)
         inv = inverse_factor(gram)
         crosst = dot(inv, zt)
-        if step < ITERS:
-            xt = dot(inverse_factor(dot(crosst, crosst, NT)), crosst)
+        if step == ITERS:
+            break
+        square = dot(crosst, crosst, NT)
+        if step == 0:
+            ahead = times_gram(crosst, parts)
+        inv = inverse_factor(square)
+        xt = dot(inv, crosst)
+        zt = dot(inv, ahead) if step == 0 else times_gram(xt, parts)
     proj_ref[...] = crosst / root
     rowt_ref[...] = dot(inv, yt) * root
 

time: 114 us -> 109 us (0.956)
  blocking collectives: 76.1 us -> 66.3 us
  starting transfers between devices: 11.1 us -> 16.9 us
    all_to_all x4, blocking collectives: 76.1 us -> 66.3 us  [exchange(): lax.all_to_all(v, 'device', 0, 0, axis_index_groups=groups, tiled=True)]
    ppermute x2, starting transfers between devices: 11.1 us -> 16.9 us  [swap(): return lax.ppermute(v, 'device', SWAP)]
where the time goes in v8:
time: 109 us
  blocking collectives  66.3 us (61%)
  Pallas kernels  21.1 us (19%)
  starting transfers between devices  16.9 us (16%)
  waiting for transfers between devices  2.18 us (2%)
  local copies, waits for them, and re-layouts  1.35 us (1%)
    all_to_all x4, blocking collectives, exchange(): lax.all_to_all(v, 'device', 0, 0, axis_index_groups=groups, tiled=True)  66.3 us
    pallas_call x1, Pallas kernels, iterate(): pl.pallas_call(functools.partial(iterate_kernel, total), out_shape=(jax.S...  18.6 us
    ppermute x2, starting transfers between devices, swap(): return lax.ppermute(v, 'device', SWAP)  16.9 us
    pallas_call x2, Pallas kernels, gram_half(): pl.pallas_call(gram_kernel, out_shape=jax.ShapeDtypeStruct((PACKED * B, B...  2.52 us
    ppermute x2, waiting for transfers between devices, swap(): return lax.ppermute(v, 'device', SWAP)  2.18 us
  transfers between devices with their start and end apart: 2, of which 1 were waited for; matrix products, arithmetic and copies ran while one was open for 0% of the time, Pallas kernels for 1%

profile of v8, /device:TPU:1, one launch (start us, length us, event | category | flops | bytes accessed | tf_op | source)
XLA Modules:
  0.0 108.6 jit_solution(3400865883071781875)
XLA Ops:
  0.6 8.8 %collective-permute-start = (f32[256,1024]{1,0:T(8,128)}, f32[256,1024]{1,0:T(8,128)S(1)}, u32[]{:S(2)}, u32[]{:S(2)}) collective-permute-start(f32[256,1024]{1,0:T(8,128)} %a_ref.3), channel_id=1, source_target_pairs={{0,4},{1,5},{2,6},{3,7},{4,0},{5,1},{6,2},{7,3},{8,12},{9,13},{10,... | collective-permute-start | bytes 3145736 | tf_op jit(solution)/shard_map/ppermute | solution.py:299
  9.5 0.0 copy-start
  9.5 1.2 %copy-done = f32[256,1024]{1,0:T(8,128)S(1)} copy-done((f32[256,1024]{1,0:T(8,128)S(1)}, f32[256,1024]{1,0:T(8,128)}, u32[]{:S(2)}) %copy-start) | copy-done | bytes 1048600
  10.7 1.3 %gram_half.2.refs_0_ = f32[2176,128]{1,0:T(8,128)S(1)} custom-call(s32[1]{0:T(128)} %bitcast.half_ref.core_ref, f32[256,1024]{1,0:T(8,128)S(1)} %copy-done), custom_call_target="tpu_custom_call" | custom-call | flops 1006632960 | bytes 2300000 | tf_op jit(solution)/shard_map/gram_half/pallas_call | solution.py:130
  11.9 0.0 collective-permute-done.a_ref
  12.0 1.3 %gram_half.3 = f32[2176,128]{1,0:T(8,128)S(1)} custom-call(s32[1]{0:T(128)} %bitcast.half_ref.core_ref, f32[256,1024]{1,0:T(8,128)S(1)} %collective-permute-done.a_ref, f32[2176,128]{1,0:T(8,128)S(1)} %gram_half.2.refs_0_), custom_call_target="tpu_custom_call" | custom-call | flops 1006632960 | bytes 2300000 | tf_op jit(solution)/shard_map/gram_half/pallas_call | solution.py:130
  13.2 19.6 %all_to_all.20 = f32[16,136,128]{2,1,0:T(8,128)S(1)} all-to-all(f32[16,136,128]{2,1,0:T(8,128)S(1)} %bitcast.7), channel_id=1, replica_groups={{0,1,2,3,8,9,10,11,64,65,66,67,72,73,74,75},{16,17,18,19,24,25,26,27,80..., dimensions={0} | all-to-all | bytes 2228224 | tf_op jit(solution)/shard_map/all_to_all | solution.py:279
  32.8 0.1 reduce_sum.27
  32.9 12.9 %all_to_all.21 = f32[4,136,128]{2,1,0:T(8,128)S(1)} all-to-all(f32[4,136,128]{2,1,0:T(8,128)S(1)} %broadcast_in_dim.9), channel_id=1, replica_groups={{0,16,32,48},{8,24,40,56},{1,17,33,49},{9,25,41,57},{2,18,34,50},{10,26..., dimensions={0} | all-to-all | bytes 557056 | tf_op jit(solution)/shard_map/all_to_all | solution.py:279
  45.9 17.6 %all_to_all.22 = f32[4,136,128]{2,1,0:T(8,128)S(1)} all-to-all(f32[4,136,128]{2,1,0:T(8,128)S(1)} %broadcast_in_dim.10), channel_id=1, replica_groups={{0,128,256,384},{64,192,320,448},{1,129,257,385},{65,193,321,449},{2,13..., dimensions={0} | all-to-all | bytes 557056 | tf_op jit(solution)/shard_map/all_to_all | solution.py:279
  63.6 0.1 broadcast_in_dim.11
  63.6 0.0 copy-start.1
  63.7 0.0 copy-start.2
  63.7 16.1 %all_to_all.23 = f32[16,136,128]{2,1,0:T(8,128)S(1)} all-to-all(f32[16,136,128]{2,1,0:T(8,128)S(1)} %broadcast_in_dim.11), channel_id=1, replica_groups={{0,1,2,3,8,9,10,11,64,65,66,67,72,73,74,75},{16,17,18,19,24,25,26,27,80..., dimensions={0} | all-to-all | bytes 2228224 | tf_op jit(solution)/shard_map/all_to_all | solution.py:279
  79.8 8.1 %collective-permute-start.1 = (f32[2176,128]{1,0:T(8,128)S(1)}, f32[2176,128]{1,0:T(8,128)S(1)}, u32[]{:S(2)}, u32[]{:S(2)}) collective-permute-start(f32[2176,128]{1,0:T(8,128)S(1)} %bitcast.5), channel_id=1, source_target_pairs={{0,4},{1,5},{2,6},{3,7},{4,0},{5,1},{6,2},{7,3},{8,12},{9,13},{10,... | collective-permute-start | bytes 3342344 | tf_op jit(solution)/shard_map/ppermute | solution.py:299
  87.8 2.2 %collective-permute-done.1.other_ref = f32[2176,128]{1,0:T(8,128)S(1)} collective-permute-done((f32[2176,128]{1,0:T(8,128)S(1)}, f32[2176,128]{1,0:T(8,128)S(1)}, u32[]{:S(2)}, u32[]{:S(2)}) %collective-permute-start.1) | collective-permute-done | bytes 1114144 | tf_op jit(solution)/shard_map/ppermute | solution.py:299
  90.0 0.0 copy-done.1
  90.0 0.0 copy-done.2
  90.0 18.6 %iterate.1 = (f32[72,256]{1,0:T(8,128)}, f32[72,1024]{1,0:T(8,128)}) custom-call(s32[1]{0:T(128)} %bitcast.half_ref.core_ref, f32[2176,128]{1,0:T(8,128)S(1)} %bitcast.6, f32[2176,128]{1,0:T(8,128)S(1)} %collective-permute-done.1.other_ref, f32[72,1024]{1,0:T(8,128)S(1)} %bitcast.8, f32[256,1024]{1,0:T(8,128)S(1)} %copy-done.1), custom_call_target="tpu_custom_call" | custom-call | tf_op jit(solution)/shard_map/iterate/pallas_call | solution.py:264
  (4 shorter events, 0.1 us)
Async XLA Ops:
  0.6 11.3 %collective-permute-start = (f32[256,1024]{1,0:T(8,128)}, f32[256,1024]{1,0:T(8,128)S(1)}, u32[]{:S(2)}, u32[]{:S(2)}) collective-permute-start(f32[256,1024]{1,0:T(8,128)} %a_ref.3), channel_id=1, source_target_pairs={{0,4},{1,5},{2,6},{3,7},{4,0},{5,1},{6,2},{7,3},{8,12},{9,13},{10,... | collective-permute-start | bytes 3145736 | tf_op jit(solution)/shard_map/ppermute | solution.py:299
  9.5 1.2 %copy-start = (f32[256,1024]{1,0:T(8,128)S(1)}, f32[256,1024]{1,0:T(8,128)}, u32[]{:S(2)}) copy-start(f32[256,1024]{1,0:T(8,128)} %a_ref.3) | copy-start | bytes 3145732
  63.6 26.4 %copy-start.1 = (f32[256,1024]{1,0:T(8,128)S(1)}, f32[256,1024]{1,0:T(8,128)}, u32[]{:S(2)}) copy-start(f32[256,1024]{1,0:T(8,128)} %a_ref.3) | copy-start | bytes 3145732
  63.7 26.4 %copy-start.2 = (f32[1024,72]{0,1:T(8,128)S(1)}, f32[1024,72]{0,1:T(8,128)}, u32[]{:S(2)}) copy-start(f32[1024,72]{0,1:T(8,128)} %param.3) | copy-start | bytes 884740
  79.8 10.3 %collective-permute-start.1 = (f32[2176,128]{1,0:T(8,128)S(1)}, f32[2176,128]{1,0:T(8,128)S(1)}, u32[]{:S(2)}, u32[]{:S(2)}) collective-permute-start(f32[2176,128]{1,0:T(8,128)S(1)} %bitcast.5), channel_id=1, source_target_pairs={{0,4},{1,5},{2,6},{3,7},{4,0},{5,1},{6,2},{7,3},{8,12},{9,13},{10,... | collective-permute-start | bytes 3342344 | tf_op jit(solution)/shard_map/ppermute | solution.py:299

commit v9 on v7

--- a/solution.py
+++ b/solution.py
@@ -12,7 +12,7 @@
 B = 128
 T = 256
 AXES = ("y", "y_pair", "z", "z_pair", "core", "x")
-NEAR = ("y_pair", "z_pair", "x")
+NEAR = ("x", "y_pair", "z_pair")
 FAR = ("z",), ("y",)
 
 NT = (((1,), (1,)), ((), ()))

time: 108 us -> 109 us (level)
  no operation moved by 1% of the time
where the time goes in v9:
time: 109 us
  blocking collectives  66.3 us (61%)
  Pallas kernels  21.1 us (19%)
  starting transfers between devices  17 us (16%)
  waiting for transfers between devices  2.18 us (2%)
  local copies, waits for them, and re-layouts  1.35 us (1%)
    all_to_all x3, blocking collectives, collect(): return lax.all_to_all(copies, axes, 0, 0, tiled=True)  46.9 us
    all_to_all x1, blocking collectives, scatter_sum(): return jnp.sum(lax.all_to_all(v, axes, 0, 0, tiled=True), axis=0)  19.4 us
    pallas_call x1, Pallas kernels, iterate(): pl.pallas_call(functools.partial(iterate_kernel, total), out_shape=(jax.S...  18.6 us
    ppermute x2, starting transfers between devices, swap(): return lax.ppermute(v, 'core', [(0, 1), (1, 0)])  17 us
    pallas_call x2, Pallas kernels, gram_half(): pl.pallas_call(gram_kernel, out_shape=jax.ShapeDtypeStruct((PACKED * B, B...  2.52 us
    ppermute x2, waiting for transfers between devices, swap(): return lax.ppermute(v, 'core', [(0, 1), (1, 0)])  2.18 us
  transfers between devices with their start and end apart: 2, of which 1 were waited for; matrix products, arithmetic and copies ran while one was open for 0% of the time, Pallas kernels for 1%

profile of v9, /device:TPU:1, one launch (start us, length us, event | category | flops | bytes accessed | tf_op | source)
XLA Modules:
  0.0 108.7 jit_solution(17945208624148903464)
XLA Ops:
  0.6 8.8 %collective-permute-start = (f32[256,1024]{1,0:T(8,128)}, f32[256,1024]{1,0:T(8,128)S(1)}, u32[]{:S(2)}, u32[]{:S(2)}) collective-permute-start(f32[256,1024]{1,0:T(8,128)} %a_ref.3), channel_id=1, source_target_pairs={{0,4},{4,0},{1,5},{5,1},{2,6},{6,2},{3,7},{7,3},{8,12},{12,8},{9,1... | collective-permute-start | bytes 3145736 | tf_op jit(solution)/shard_map/ppermute | solution.py:267
  9.4 0.0 copy-start
  9.4 1.2 %copy-done = f32[256,1024]{1,0:T(8,128)S(1)} copy-done((f32[256,1024]{1,0:T(8,128)S(1)}, f32[256,1024]{1,0:T(8,128)}, u32[]{:S(2)}) %copy-start) | copy-done | bytes 1048600
  10.7 1.3 %gram_half.2.refs_0_ = f32[2176,128]{1,0:T(8,128)S(1)} custom-call(s32[1]{0:T(128)} %bitcast.half_ref.core_ref, f32[256,1024]{1,0:T(8,128)S(1)} %copy-done), custom_call_target="tpu_custom_call" | custom-call | flops 1006632960 | bytes 2300000 | tf_op jit(solution)/shard_map/gram_half/pallas_call | solution.py:101
  11.9 0.0 collective-permute-done.a_ref
  11.9 1.3 %gram_half.3 = f32[2176,128]{1,0:T(8,128)S(1)} custom-call(s32[1]{0:T(128)} %bitcast.half_ref.core_ref, f32[256,1024]{1,0:T(8,128)S(1)} %collective-permute-done.a_ref, f32[2176,128]{1,0:T(8,128)S(1)} %gram_half.2.refs_0_), custom_call_target="tpu_custom_call" | custom-call | flops 1006632960 | bytes 2300000 | tf_op jit(solution)/shard_map/gram_half/pallas_call | solution.py:101
  13.2 19.4 %all_to_all.20 = f32[16,136,128]{2,1,0:T(8,128)S(1)} all-to-all(f32[16,136,128]{2,1,0:T(8,128)S(1)} %bitcast.7), channel_id=1, replica_groups=mesh['y'=4,'y_pair'=2,'z'=4,'z_pair'=2,'core'=2,'x'=4] {'x','y_pair','z_..., dimensions={0} | all-to-all | bytes 2228224 | tf_op jit(solution)/shard_map/all_to_all | solution.py:251
  32.6 0.1 reduce_sum.27
  32.7 15.6 %all_to_all.21 = f32[4,136,128]{2,1,0:T(8,128)S(1)} all-to-all(f32[4,136,128]{2,1,0:T(8,128)S(1)} %broadcast_in_dim.9), channel_id=1, replica_groups=mesh['y'=4,'y_pair'=2,'z'=4,'z_pair'=2,'core'=2,'x'=4] {'z'}, dimensions={0} | all-to-all | bytes 557056 | tf_op jit(solution)/shard_map/all_to_all | solution.py:256
  48.4 15.2 %all_to_all.22 = f32[4,136,128]{2,1,0:T(8,128)S(1)} all-to-all(f32[4,136,128]{2,1,0:T(8,128)S(1)} %broadcast_in_dim.10), channel_id=1, replica_groups=mesh['y'=4,'y_pair'=2,'z'=4,'z_pair'=2,'core'=2,'x'=4] {'y'}, dimensions={0} | all-to-all | bytes 557056 | tf_op jit(solution)/shard_map/all_to_all | solution.py:256
  63.7 0.1 broadcast_in_dim.11
  63.7 0.0 copy-start.1
  63.7 0.0 copy-start.2
  63.8 16.0 %all_to_all.23 = f32[16,136,128]{2,1,0:T(8,128)S(1)} all-to-all(f32[16,136,128]{2,1,0:T(8,128)S(1)} %broadcast_in_dim.11), channel_id=1, replica_groups=mesh['y'=4,'y_pair'=2,'z'=4,'z_pair'=2,'core'=2,'x'=4] {'x','y_pair','z_..., dimensions={0} | all-to-all | bytes 2228224 | tf_op jit(solution)/shard_map/all_to_all | solution.py:256
  79.8 8.2 %collective-permute-start.1 = (f32[2176,128]{1,0:T(8,128)S(1)}, f32[2176,128]{1,0:T(8,128)S(1)}, u32[]{:S(2)}, u32[]{:S(2)}) collective-permute-start(f32[2176,128]{1,0:T(8,128)S(1)} %bitcast.5), channel_id=1, source_target_pairs={{0,4},{4,0},{1,5},{5,1},{2,6},{6,2},{3,7},{7,3},{8,12},{12,8},{9,1... | collective-permute-start | bytes 3342344 | tf_op jit(solution)/shard_map/ppermute | solution.py:267
  88.0 2.2 %collective-permute-done.1.other_ref = f32[2176,128]{1,0:T(8,128)S(1)} collective-permute-done((f32[2176,128]{1,0:T(8,128)S(1)}, f32[2176,128]{1,0:T(8,128)S(1)}, u32[]{:S(2)}, u32[]{:S(2)}) %collective-permute-start.1) | collective-permute-done | bytes 1114144 | tf_op jit(solution)/shard_map/ppermute | solution.py:267
  90.1 0.0 copy-done.1
  90.1 0.0 copy-done.2
  90.1 18.6 %iterate.1 = (f32[72,256]{1,0:T(8,128)}, f32[72,1024]{1,0:T(8,128)}) custom-call(s32[1]{0:T(128)} %bitcast.half_ref.core_ref, f32[2176,128]{1,0:T(8,128)S(1)} %bitcast.6, f32[2176,128]{1,0:T(8,128)S(1)} %collective-permute-done.1.other_ref, f32[72,1024]{1,0:T(8,128)S(1)} %bitcast.8, f32[256,1024]{1,0:T(8,128)S(1)} %copy-done.1), custom_call_target="tpu_custom_call" | custom-call | tf_op jit(solution)/shard_map/iterate/pallas_call | solution.py:235
  (4 shorter events, 0.1 us)
Async XLA Ops:
  0.6 11.3 %collective-permute-start = (f32[256,1024]{1,0:T(8,128)}, f32[256,1024]{1,0:T(8,128)S(1)}, u32[]{:S(2)}, u32[]{:S(2)}) collective-permute-start(f32[256,1024]{1,0:T(8,128)} %a_ref.3), channel_id=1, source_target_pairs={{0,4},{4,0},{1,5},{5,1},{2,6},{6,2},{3,7},{7,3},{8,12},{12,8},{9,1... | collective-permute-start | bytes 3145736 | tf_op jit(solution)/shard_map/ppermute | solution.py:267
  9.4 1.2 %copy-start = (f32[256,1024]{1,0:T(8,128)S(1)}, f32[256,1024]{1,0:T(8,128)}, u32[]{:S(2)}) copy-start(f32[256,1024]{1,0:T(8,128)} %a_ref.3) | copy-start | bytes 3145732
  63.7 26.4 %copy-start.1 = (f32[256,1024]{1,0:T(8,128)S(1)}, f32[256,1024]{1,0:T(8,128)}, u32[]{:S(2)}) copy-start(f32[256,1024]{1,0:T(8,128)} %a_ref.3) | copy-start | bytes 3145732
  63.7 26.4 %copy-start.2 = (f32[1024,72]{0,1:T(8,128)S(1)}, f32[1024,72]{0,1:T(8,128)}, u32[]{:S(2)}) copy-start(f32[1024,72]{0,1:T(8,128)} %param.3) | copy-start | bytes 884740
  79.8 10.4 %collective-permute-start.1 = (f32[2176,128]{1,0:T(8,128)S(1)}, f32[2176,128]{1,0:T(8,128)S(1)}, u32[]{:S(2)}, u32[]{:S(2)}) collective-permute-start(f32[2176,128]{1,0:T(8,128)S(1)} %bitcast.5), channel_id=1, source_target_pairs={{0,4},{4,0},{1,5},{5,1},{2,6},{6,2},{3,7},{7,3},{8,12},{12,8},{9,1... | collective-permute-start | bytes 3342344 | tf_op jit(solution)/shard_map/ppermute | solution.py:267
